TPU v7x, 256 devices: a whole 4x4x8 slice. The times are simulated.
256 devices in a mesh: leaf: 64 (over z, x, core), rhs: 4 (over y).
Axes of the slice: x: 4, y: 4, z: 8, core: 2. Of those that a mesh axis runs over, the one named last changes fastest.
Arguments:
- rhs_block: bfloat16 [256, 131072], P('rhs', 'leaf'), may hold values from -6 to 6
- leaf_basis: bfloat16 [131072, 128], P('leaf'), may hold values from -0.5 to 0.5
- local_transfer: bfloat16 [64, 30, 128, 128], P('leaf'), may hold values from -0.375 to 0.375
- top_transfer: bfloat16 [120, 128, 128], replicated, may hold values from -0.375 to 0.375
- coupling_tiles: bfloat16 [64, 128, 128], P('rhs'), may hold values from -0.1875 to 0.1875
- send_index: int32 [64, 64, 4], replicated, may hold values from -1 to 15, as said below
- leaf_list: int32 [2, 1024, 192], P(None, 'leaf'), may hold values from 0 to 255, as said below
- top_list: int32 [3, 512], replicated, may hold values from 0 to 127, as said below
Outputs:
- far_field: bfloat16 [256, 131072], P('rhs', 'leaf')
Inputs may be any that keep to these rules, and one draw needn't show every extreme that they name: `send_index`: each slot holds a distinct local leaf of the sender or -1; the used slots of a pair come first and the rest are -1; every device fills all 4 slots to itself. `leaf_list`: every slot named in [0] holds a leaf (not -1) for the receiving device that owns the target leaf. `top_list`: target and source lie on the same level of the top tree, at least level 2, and differ by two or more places cyclically within it.
All inputs are finite; a program needn't handle non-finite values.
Results may differ from a plain program's by a relative error of at most 0.017.
Values may be sent and summed in bfloat16 or wider, within the bound.
No kernel may reach another device: no remote copies, remote signals or barrier semaphores. Data moves between devices by JAX's collectives and lax.ppermute only.
A program may use at most 192 MiB of HBM per device.

v0:
```python
import functools

import jax
import jax.numpy as jnp
from jax import lax
from jax.experimental import pallas as pl
from jax.experimental.pallas import tpu as pltpu
from jax.sharding import Mesh, PartitionSpec as P

F32 = jnp.float32
BF16 = jnp.bfloat16
RANK = 128
LD = 16
TILES = 64
GROUP = 16
ROWS = 4
TARGETS = 48
LANES = ROWS * RANK
VMEM_LIMIT = 60 * 1024 * 1024


def mm(a, b):
    return jnp.dot(a, b, preferred_element_type=F32)


def mm_nt(a, b):
    return lax.dot_general(a, b, (((1,), (1,)), ((), ())), preferred_element_type=F32)


def gather_kernel(xme, rhs, basis, trans, lists, msg, panels, root):
    x = xme[0]
    current = []
    for g in range(LD):
        panel = mm(rhs[:, g * RANK : (g + 1) * RANK], basis[g * RANK : (g + 1) * RANK, :])
        panels[g * 64 : (g + 1) * 64, :] = panel
        current.append(panel.astype(BF16))
    count = LD
    while count > 1:
        above = []
        for h in range(count // 2):
            pair = jnp.concatenate([current[2 * h], current[2 * h + 1]], axis=1)
            at = count - 2 + 2 * h
            above.append(mm(pair, trans[at : at + 2].reshape(2 * RANK, RANK)))
        current = [a.astype(BF16) for a in above]
        count //= 2
    root[...] = jnp.zeros_like(root)
    root[0:64, :] = above[0]
    slot = lists[0]
    p = slot >> 2
    slot = ((x - (p >> 1)) & 3) * 64 + (p >> 3) * 8 + (p & 1) * 4 + (slot & 3)
    slot = slot.astype(F32).astype(BF16)
    tile = lists[1].astype(F32).astype(BF16)
    none = jnp.full((LD, RANK), -1.0, BF16)
    for j in range(GROUP):
        msg[j, :, 128:256] = none
        msg[j, :, 0:192] = slot
        msg[j, :, 384:512] = none
        msg[j, :, 256:448] = tile
        for r in range(ROWS):
            msg[j, :, 512 + r * RANK : 512 + (r + 1) * RANK] = panels[
                pl.ds(r * GROUP + j, LD, stride=64), :
            ].astype(BF16)
        msg[j, :, 1024:1152] = root[pl.ds(j, 16, stride=16), :].astype(BF16)


def tally_kernel(xme, lists, picks, top, counts, sel, top_counts, low, high):
    d = pl.program_id(0)
    x = xme[0]
    codes = lists[0].astype(F32)
    slot_ids = lax.broadcasted_iota(jnp.int32, (256, 256), 0).astype(F32)
    tile_ids = lax.broadcasted_iota(jnp.int32, (TILES, 256), 0).astype(F32)
    for g in range(LD):
        slot_hot = jnp.where(codes[g : g + 1, 0:256] == slot_ids, 1.0, 0.0).astype(BF16)
        tile_hot = jnp.where(codes[g : g + 1, 256:512] == tile_ids, 1.0, 0.0).astype(BF16)
        tally = mm_nt(tile_hot, slot_hot)
        low[pl.ds(g, TILES, stride=LD), :] = tally[:, 0:128]
        high[pl.ds(g, TILES, stride=LD), :] = tally[:, 128:256]
    counts[0, :, 0:128] = low[...].astype(BF16)
    counts[0, :, 128:256] = high[...].astype(BF16)

    @pl.when(d == 0)
    def _():
        lane = lax.broadcasted_iota(jnp.int32, (256, 256), 1)
        for t in range(GROUP):
            hot = jnp.where(picks[:, t : t + 1] == lane, 1.0, 0.0).astype(BF16)
            for s in range(4):
                sel[s, t * 64 : (t + 1) * 64, :] = hot[s * 64 : (s + 1) * 64, :]

    @pl.when(d == 1)
    def _():
        n = top[0:1, :]
        source = top[1:2, :]
        tile = top[2:3, :]
        at = jnp.where(n < 8, n - 4, n - 4)
        m16 = n - 16
        at = jnp.where(n >= 16, jnp.where((m16 & 1) == (x >> 1), 12 + (m16 >> 1), -1), at)
        m32 = n - 32
        at = jnp.where(n >= 32, jnp.where((m32 & 3) == x, 20 + (m32 >> 2), -1), at)
        m64 = n - 64
        at = jnp.where(
            n >= 64,
            jnp.where(((m64 >> 1) & 3) == x, 28 + (m64 >> 3) * 2 + (m64 & 1), -1),
            at,
        )
        code = jnp.where(at >= 0, tile * TARGETS + at, -1)
        width = top.shape[1]
        node = lax.broadcasted_iota(jnp.int32, (128, width), 0)
        source_hot = jnp.where(source == node, 1.0, 0.0).astype(BF16)
        part = 8 * TARGETS
        rows = lax.broadcasted_iota(jnp.int32, (part, width), 0)
        for b in range(8):
            hot = jnp.where(code == rows + b * part, 1.0, 0.0).astype(BF16)
            top_counts[b * part : (b + 1) * part, :] = mm_nt(hot, source_hot).astype(BF16)


def couple_kernel(
    xme, a0, a1, a2, a3, sel, counts, top_counts, table, tt, msg, pool, zs, xtop, acc, root
):
    d = pl.program_id(0)
    x = xme[0]
    blocks = (a0, a1, a2, a3)
    total = 256 + TARGETS

    @pl.when(d == 0)
    def _():
        for s in range(4):
            panels = blocks[s][:, :, 0:LANES].reshape(256, LANES)
            for m in range(4):
                got = mm(sel[s, m * 256 : (m + 1) * 256, :], panels).astype(BF16)
                for t in range(4):
                    pool[m * 4 + t, s * 64 : (s + 1) * 64, :] = got[t * 64 : (t + 1) * 64, :]

    for m in range(4):
        z = mm(counts[0, m * 256 : (m + 1) * 256, :], pool[d]).astype(BF16)
        zs[m * 16 : (m + 1) * 16, d] = z.reshape(16, 16, LANES)

    @pl.when(d == GROUP - 1)
    def _():
        xtop[...] = jnp.zeros_like(xtop)
        for s in range(4):
            for q in range(GROUP):
                n = 64 + (q >> 1) * 8 + ((x - s) & 3) * 2 + (q & 1)
                xtop[pl.ds(n, ROWS, stride=128), :] = blocks[s][q, :, LANES:].astype(F32)[0:ROWS]
        for n in range(63, 3, -1):
            left = xtop[pl.ds(2 * n, ROWS, stride=128), :]
            right = xtop[pl.ds(2 * n + 1, ROWS, stride=128), :]
            pair = jnp.concatenate([left, right], axis=1).astype(BF16)
            up = mm(pair, tt[2 * n - 8 : 2 * n - 6].reshape(2 * RANK, RANK))
            xtop[pl.ds(n, ROWS, stride=128), :] = up.astype(BF16).astype(F32)
        sources = jnp.concatenate(
            [xtop[r * 128 : (r + 1) * 128, :] for r in range(ROWS)], axis=1
        ).astype(BF16)
        part = 8 * TARGETS
        for b in range(8):
            z = mm(top_counts[b * part : (b + 1) * part, :], sources).astype(BF16)
            zs[b * 8 : (b + 1) * 8, 16:19] = z.reshape(8, 3, 16, LANES)
        acc[...] = jnp.zeros_like(acc)

        def step(i, carry):
            for r in range(ROWS):
                lanes = slice(r * RANK, (r + 1) * RANK)
                done = None
                for h in range(2):
                    k = i * 4 + h * 2
                    both = jnp.concatenate(
                        [
                            zs[k, :, :, lanes].reshape(total, RANK),
                            zs[k + 1, :, :, lanes].reshape(total, RANK),
                        ],
                        axis=1,
                    )
                    term = mm(both, table[pl.ds(k, 2)].reshape(2 * RANK, RANK))
                    done = term if done is None else done + term
                acc[r * total : (r + 1) * total, :] += done
            return carry

        lax.fori_loop(0, TILES // 4, step, 0)

        def get(t):
            return acc[pl.ds(256 + t, ROWS, stride=total), :]

        def add(t, value):
            acc[pl.ds(256 + t, ROWS, stride=total), :] += value

        for i in range(4):
            y = mm_nt(get(i).astype(BF16), tt[2 * i : 2 * i + 2].reshape(2 * RANK, RANK))
            add(4 + 2 * i, y[:, 0:RANK])
            add(5 + 2 * i, y[:, RANK:])
        for z in range(8):
            add(12 + z, mm_nt(get(4 + z).astype(BF16), tt[8 + z * 2 + (x >> 1)]))
        for z in range(8):
            add(20 + z, mm_nt(get(12 + z).astype(BF16), tt[24 + z * 4 + x]))
        for z in range(8):
            pair = tt[pl.ds(56 + z * 8 + x * 2, 2)].reshape(2 * RANK, RANK)
            y = mm_nt(get(20 + z).astype(BF16), pair)
            add(28 + 2 * z, y[:, 0:RANK])
            add(29 + 2 * z, y[:, RANK:])
        root[...] = jnp.zeros_like(root)
        for q in range(GROUP):
            for r in range(ROWS):
                msg[q, :, r * RANK : (r + 1) * RANK] = acc[
                    r * total + q * 16 : r * total + (q + 1) * 16, :
                ].astype(BF16)
            root[q * 16 : q * 16 + ROWS, :] = get(28 + q)
            msg[q, :, LANES:] = root[q * 16 : (q + 1) * 16, :].astype(BF16)


def spread_kernel(msg, basis, trans, out, panels, root):
    for j in range(GROUP):
        for r in range(ROWS):
            panels[r * 256 + j * 16 : r * 256 + (j + 1) * 16, :] = msg[
                j, :, r * RANK : (r + 1) * RANK
            ].astype(F32)
        root[pl.ds(j, ROWS, stride=GROUP), :] = msg[j, :, LANES:].astype(F32)[0:ROWS]
    current = [root[...]]
    count = 2
    while count <= LD:
        below = []
        for h in range(count // 2):
            at = count - 2 + 2 * h
            y = mm_nt(current[h].astype(BF16), trans[at : at + 2].reshape(2 * RANK, RANK))
            below += [y[:, 0:RANK], y[:, RANK:]]
        current = below
        count *= 2
    for g in range(LD):
        coupled = jnp.concatenate(
            [panels[pl.ds(r * 256 + g, GROUP, stride=16), :] for r in range(ROWS)], axis=0
        )
        w = (current[g] + coupled).astype(BF16)
        out[:, g * RANK : (g + 1) * RANK] = mm_nt(w, basis[g * RANK : (g + 1) * RANK, :]).astype(
            BF16
        )


SMEM = pl.BlockSpec(memory_space=pltpu.SMEM)
WHOLE = pl.BlockSpec(memory_space=pltpu.VMEM)


def params():
    return pltpu.CompilerParams(vmem_limit_bytes=VMEM_LIMIT)


def fixed(shape):
    return pl.BlockSpec(shape, lambda d: (0,) * len(shape), pipeline_mode=pl.Buffered(1))


def cost(flops, moved):
    return pl.CostEstimate(flops=flops, bytes_accessed=moved, transcendentals=0)


def shards(
    rhs_block,
    leaf_basis,
    local_transfer,
    top_transfer,
    coupling_tiles,
    send_index,
    leaf_list,
    top_list,
):
    x = lax.axis_index("x")
    xme = x.astype(jnp.int32).reshape(1)
    trans = local_transfer.reshape(30, RANK, RANK)
    table = lax.all_gather(coupling_tiles, "rhs", axis=0, tiled=True)
    msg = pl.pallas_call(
        gather_kernel,
        out_shape=jax.ShapeDtypeStruct((GROUP, LD, 1152), BF16),
        in_specs=[SMEM] + [WHOLE] * 4,
        out_specs=WHOLE,
        scratch_shapes=[pltpu.VMEM((1024, RANK), F32), pltpu.VMEM((256, RANK), F32)],
        compiler_params=params(),
        name="leaf_panels",
    )(xme, rhs_block, leaf_basis, trans, leaf_list)
    msg = lax.all_to_all(msg, ("z", "core"), 0, 0, tiled=True)
    mine = msg[:, :, 512:1152]
    blocks = [mine] + [
        lax.ppermute(mine, "x", [(i, (i + s) % 4) for i in range(4)]) for s in (1, 2, 3)
    ]
    index = send_index.reshape(8, 4, 2, 8, 4, 2, 4)
    index = lax.dynamic_index_in_dim(index, x, 4, keepdims=False)
    index = jnp.concatenate(
        [lax.dynamic_slice_in_dim(index, (x - s) % 4, 1, 1) for s in range(4)], axis=1
    )
    index = index.transpose(1, 0, 2, 5, 3, 4)
    place = (jnp.arange(8)[:, None] * 2 + jnp.arange(2)[None, :])[None, :, :, None, None, None]
    picks = jnp.where(index >= 0, index + 16 * place, -1).reshape(256, GROUP).astype(jnp.int32)
    counts, sel, top_counts = pl.pallas_call(
        tally_kernel,
        grid=(GROUP,),
        out_shape=(
            jax.ShapeDtypeStruct((GROUP, 1024, 256), BF16),
            jax.ShapeDtypeStruct((4, 1024, 256), BF16),
            jax.ShapeDtypeStruct((TILES * TARGETS, 128), BF16),
        ),
        in_specs=[
            SMEM,
            pl.BlockSpec((1, LD, 512), lambda d: (d, 0, 0)),
            fixed((256, GROUP)),
            fixed(top_list.shape),
        ],
        out_specs=(
            pl.BlockSpec((1, 1024, 256), lambda d: (d, 0, 0)),
            pl.BlockSpec((4, 1024, 256), lambda d: (0, 0, 0)),
            pl.BlockSpec((TILES * TARGETS, 128), lambda d: (0, 0)),
        ),
        scratch_shapes=[pltpu.VMEM((1024, 128), F32)] * 2,
        compiler_params=params(),
        cost_estimate=cost(4_000_000_000, 12_000_000),
        name="tallies",
    )(xme, msg, picks, top_list)
    total = 256 + TARGETS
    back = pl.pallas_call(
        couple_kernel,
        grid=(GROUP,),
        out_shape=jax.ShapeDtypeStruct((GROUP, LD, 640), BF16),
        in_specs=[SMEM]
        + [fixed((GROUP, LD, 640))] * 4
        + [
            fixed((4, 1024, 256)),
            pl.BlockSpec((1, 1024, 256), lambda d: (d, 0, 0)),
            fixed((TILES * TARGETS, 128)),
            fixed((TILES, RANK, RANK)),
            fixed((120, RANK, RANK)),
        ],
        out_specs=pl.BlockSpec((GROUP, LD, 640), lambda d: (0, 0, 0)),
        scratch_shapes=[
            pltpu.VMEM((GROUP, 256, LANES), BF16),
            pltpu.VMEM((TILES, 19, 16, LANES), BF16),
            pltpu.VMEM((ROWS * 128, RANK), F32),
            pltpu.VMEM((ROWS * total, RANK), F32),
            pltpu.VMEM((GROUP * 16, RANK), F32),
        ],
        compiler_params=params(),
        cost_estimate=cost(8_000_000_000, 20_000_000),
        name="interactions",
    )(xme, *blocks, sel, counts, top_counts, table, top_transfer)
    back = lax.all_to_all(back, ("z", "core"), 0, 0, tiled=True)
    return pl.pallas_call(
        spread_kernel,
        out_shape=jax.ShapeDtypeStruct(rhs_block.shape, BF16),
        in_specs=[WHOLE] * 3,
        out_specs=WHOLE,
        scratch_shapes=[pltpu.VMEM((1024, RANK), F32), pltpu.VMEM((64, RANK), F32)],
        compiler_params=params(),
        name="far_field",
    )(back, leaf_basis, trans)


def solution(mesh):
    grid = Mesh(mesh.devices.reshape(8, 4, 2, 4), ("z", "x", "core", "rhs"))
    leaf = ("z", "x", "core")
    placed = (
        P("rhs", leaf),
        P(leaf, None),
        P(leaf, None, None, None),
        P(),
        P("rhs", None, None),
        P(),
        P(None, leaf, None),
        P(),
    )
    return jax.shard_map(
        shards, mesh=grid, in_specs=placed, out_specs=P("rhs", leaf), check_vma=False
    )
```

profile of v0, /device:TPU:1, one launch (start us, length us, event | category | flops | bytes accessed | tf_op | source)
XLA Modules:
  0.0 120.0 jit_solution(14417578961181635887)
XLA Ops:
  6.5 0.0 all-gather.2.cloned.1.call-start
  6.5 0.7 all-gather.2.cloned.1.call-update
  7.3 3.3 %leaf_panels.1 = bf16[16,16,1152]{2,1,0:T(8,128)(2,1)} custom-call(s32[1]{0:T(128)} %bitcast.xme, bf16[64,2048]{1,0:T(8,128)(2,1)} %rhs.1, bf16[2048,128]{1,0:T(8,128)(2,1)} %basis.3, bf16[30,128,128]{2,1,0:T(8,128)(2,1)} %bitcast.11, s32[2,16,192]{2,1,0:T(8,128)} %lists.1), custom_call_target="tpu_custom_call" | custom-call | tf_op jit(solution)/shard_map/leaf_panels/pallas_call | solution.py:265
  10.5 10.0 %all-to-all-start = ((bf16[16,16,1152]{2,1,0:T(8,128)(2,1)}), bf16[16,16,1152]{2,1,0:T(8,128)(2,1)S(1)}, u32[]{:S(2)}, u32[]{:S(2)}) async-start(bf16[16,16,1152]{2,1,0:T(8,128)(2,1)} %leaf_panels.1), calls=%async_computation | async-start | bytes 1179648 | tf_op jit(solution)/shard_map/all_to_all | solution.py:274
  20.5 0.0 copy-done.2
  20.5 0.7 copy.18
  21.2 0.2 constant_dynamic-slice_fusion.3
  21.4 0.3 copy.19
  21.7 0.3 copy.20
  22.0 0.3 copy.21
  22.2 0.3 copy.22
  22.6 0.1 select_bitcast_fusion
  22.7 1.0 copy.23
  23.7 0.7 reshape.48
  24.4 0.8 copy.24.picks
  25.1 14.1 %all-to-all-done.lists = bf16[16,16,1152]{2,1,0:T(8,128)(2,1)S(1)} async-done(((bf16[16,16,1152]{2,1,0:T(8,128)(2,1)}), bf16[16,16,1152]{2,1,0:T(8,128)(2,1)S(1)}, u32[]{:S(2)}, u32[]{:S(2)}) %all-to-all-start) | async-done | bytes 589856 | tf_op jit(solution)/shard_map/all_to_all | solution.py:274
  39.2 0.0 copy-start.1
  39.2 1.3 %collective-permute-start = (bf16[16,16,640]{2,1,0:T(8,128)(2,1)S(1)}, bf16[16,16,640]{2,1,0:T(8,128)(2,1)S(1)}, u32[]{:S(2)}, u32[]{:S(2)}) collective-permute-start(bf16[16,16,640]{2,1,0:T(8,128)(2,1)S(1)} %slice.4.a0), channel_id=1, source_target_pairs={{0,8},{8,16},{16,24},{24,0},{1,9},{9,17},{17,25},{25,1},{2,10},{10... | collective-permute-start | bytes 983048 | tf_op jit(solution)/shard_map/ppermute | solution.py:277
  40.5 2.4 %collective-permute-start.1 = (bf16[16,16,640]{2,1,0:T(8,128)(2,1)S(1)}, bf16[16,16,640]{2,1,0:T(8,128)(2,1)S(1)}, u32[]{:S(2)}, u32[]{:S(2)}) collective-permute-start(bf16[16,16,640]{2,1,0:T(8,128)(2,1)S(1)} %slice.4.a0), channel_id=1, source_target_pairs={{0,16},{8,24},{16,0},{24,8},{1,17},{9,25},{17,1},{25,9},{2,18},{10... | collective-permute-start | bytes 983048 | tf_op jit(solution)/shard_map/ppermute | solution.py:277
  43.0 1.2 collective-permute-start.2
  44.1 0.0 copy-done
  44.1 19.5 %tallies.1 = (bf16[16,1024,256]{2,1,0:T(8,128)(2,1)}, bf16[4,1024,256]{2,1,0:T(8,128)(2,1)}, bf16[3072,128]{1,0:T(8,128)(2,1)}) custom-call(s32[1]{0:T(128)} %bitcast.xme, bf16[16,16,1152]{2,1,0:T(8,128)(2,1)} %copy-done, s32[256,16]{1,0:T(8,128)} %copy.24.picks, s32[3,512]{1,0:T(4,128)} %top.1), custom_call_target="tpu_custom_call" | custom-call | flops 4000000000 | bytes 12000000 | tf_op jit(solution)/shard_map/tallies/pallas_call | solution.py:287
  63.6 0.0 collective-permute-done.a1
  63.6 0.0 collective-permute-done.1.a2
  63.7 0.0 collective-permute-done.2.a3
  63.7 0.0 all-gather.2.cloned.1.call-done.table
  63.7 0.7 copy-done.3
  64.4 0.1 copy-done.4
  64.5 0.1 copy-done.5
  64.6 28.3 %interactions.1 = bf16[16,16,640]{2,1,0:T(8,128)(2,1)} custom-call(s32[1]{0:T(128)} %bitcast.xme, bf16[16,16,640]{2,1,0:T(8,128)(2,1)} %copy-done.1, bf16[16,16,640]{2,1,0:T(8,128)(2,1)} %copy-done.3, bf16[16,16,640]{2,1,0:T(8,128)(2,1)} %copy-done.4, bf16[16,16,640]{2,1,0:T(8,128)(2,1)} %copy-done.5, bf16[4,1024,256]{2,1,0:T(8,128)(2,1)} %get-tuple-element.8.sel, ...), custom_call_target="tpu_custom_call" | custom-call | flops 8000000000 | bytes 20000000 | tf_op jit(solution)/shard_map/interactions/pallas_call | solution.py:312
  92.9 17.1 %all_to_all.10.msg = bf16[16,16,640]{2,1,0:T(8,128)(2,1)} all-to-all(bf16[16,16,640]{2,1,0:T(8,128)(2,1)} %interactions.1), channel_id=1, replica_groups=mesh['z'=8,'x'=4,'core'=2,'rhs'=4] {'z','core'}, dimensions={0} | all-to-all | bytes 655360 | tf_op jit(solution)/shard_map/all_to_all | solution.py:337
  110.0 3.2 %far_field.1 = bf16[64,2048]{1,0:T(8,128)(2,1)} custom-call(bf16[16,16,640]{2,1,0:T(8,128)(2,1)} %all_to_all.10.msg, bf16[2048,128]{1,0:T(8,128)(2,1)} %basis.3, bf16[30,128,128]{2,1,0:T(8,128)(2,1)} %bitcast.12), custom_call_target="tpu_custom_call" | custom-call | tf_op jit(solution)/shard_map/far_field/pallas_call | solution.py:338
  (9 shorter events, 0.1 us)
Async XLA Ops:
  6.5 14.0 %copy-start.2 = (s32[64,64,4]{1,2,0:T(4,128)S(1)}, s32[64,64,4]{1,2,0:T(4,128)}, u32[]{:S(2)}) copy-start(s32[64,64,4]{1,2,0:T(4,128)} %param.13) | copy-start | bytes 196612
  6.5 57.2 %all-gather.2.cloned.1.call-start = ((), (), s32[]{:S(2)}) async-start(), calls=%async_computation.2 | async-start | bytes 2621440 | tf_op jit(solution)/shard_map/all_gather | solution.py:264
  10.5 28.6 %all-to-all-start = ((bf16[16,16,1152]{2,1,0:T(8,128)(2,1)}), bf16[16,16,1152]{2,1,0:T(8,128)(2,1)S(1)}, u32[]{:S(2)}, u32[]{:S(2)}) async-start(bf16[16,16,1152]{2,1,0:T(8,128)(2,1)} %leaf_panels.1), calls=%async_computation | async-start | bytes 1179648 | tf_op jit(solution)/shard_map/all_to_all | solution.py:274
  39.2 4.9 %copy-start = (bf16[16,16,1152]{2,1,0:T(8,128)(2,1)}, bf16[16,16,1152]{2,1,0:T(8,128)(2,1)S(1)}, u32[]{:S(2)}) copy-start(bf16[16,16,1152]{2,1,0:T(8,128)(2,1)S(1)} %all-to-all-done.lists) | copy-start | bytes 1769476
  39.2 24.4 %copy-start.1 = (bf16[16,16,640]{2,1,0:T(8,128)(2,1)}, bf16[16,16,640]{2,1,0:T(8,128)(2,1)S(1)}, u32[]{:S(2)}) copy-start(bf16[16,16,640]{2,1,0:T(8,128)(2,1)S(1)} %slice.4.a0) | copy-start | bytes 983044
  39.2 24.4 %collective-permute-start = (bf16[16,16,640]{2,1,0:T(8,128)(2,1)S(1)}, bf16[16,16,640]{2,1,0:T(8,128)(2,1)S(1)}, u32[]{:S(2)}, u32[]{:S(2)}) collective-permute-start(bf16[16,16,640]{2,1,0:T(8,128)(2,1)S(1)} %slice.4.a0), channel_id=1, source_target_pairs={{0,8},{8,16},{16,24},{24,0},{1,9},{9,17},{17,25},{25,1},{2,10},{10... | collective-permute-start | bytes 983048 | tf_op jit(solution)/shard_map/ppermute | solution.py:277
  40.5 23.1 %collective-permute-start.1 = (bf16[16,16,640]{2,1,0:T(8,128)(2,1)S(1)}, bf16[16,16,640]{2,1,0:T(8,128)(2,1)S(1)}, u32[]{:S(2)}, u32[]{:S(2)}) collective-permute-start(bf16[16,16,640]{2,1,0:T(8,128)(2,1)S(1)} %slice.4.a0), channel_id=1, source_target_pairs={{0,16},{8,24},{16,0},{24,8},{1,17},{9,25},{17,1},{25,9},{2,18},{10... | collective-permute-start | bytes 983048 | tf_op jit(solution)/shard_map/ppermute | solution.py:277
  43.0 20.7 %collective-permute-start.2 = (bf16[16,16,640]{2,1,0:T(8,128)(2,1)S(1)}, bf16[16,16,640]{2,1,0:T(8,128)(2,1)S(1)}, u32[]{:S(2)}, u32[]{:S(2)}) collective-permute-start(bf16[16,16,640]{2,1,0:T(8,128)(2,1)S(1)} %slice.4.a0), channel_id=1, source_target_pairs={{0,24},{8,0},{16,8},{24,16},{1,25},{9,1},{17,9},{25,17},{2,26},{10... | collective-permute-start | bytes 983048 | tf_op jit(solution)/shard_map/ppermute | solution.py:277
  63.6 0.7 copy-start.3
  63.7 0.8 copy-start.4
  63.7 0.9 copy-start.5
Sparse Core Ops, SparseCore 0:
  9.2 37.2 all-gather.1
where the time goes:
time: 121 us; the launch traced here: 120 us
  Pallas kernels  54.3 us (45%)
  blocking collectives  17.1 us (14%)
  starting transfers between devices  14.9 us (12%)
  waiting for transfers between devices  14.8 us (12%)
  between operations  13.5 us (11%)
  local copies, waits for them, and re-layouts  5.34 us (4%)
    pallas_call x1, Pallas kernels, shards(): pl.pallas_call(couple_kernel, grid=(GROUP,), out_shape=jax.ShapeDtypeStru...  28.3 us
    pallas_call x1, Pallas kernels, shards(): pl.pallas_call(tally_kernel, grid=(GROUP,), out_shape=(jax.ShapeDtypeStru...  19.5 us
    all_to_all x1, blocking collectives, shards(): back = lax.all_to_all(back, ('z', 'core'), 0, 0, tiled=True)  17.1 us
    all_to_all x1, waiting for transfers between devices, shards(): msg = lax.all_to_all(msg, ('z', 'core'), 0, 0, tiled=True)  14.1 us
    all_to_all x1, starting transfers between devices, shards(): msg = lax.all_to_all(msg, ('z', 'core'), 0, 0, tiled=True)  9.98 us
    ppermute x3, starting transfers between devices, shards(): lax.ppermute(mine, 'x', [(i, (i + s) % 4) for i in range(4)])  4.89 us
    pallas_call x1, Pallas kernels, shards(): pl.pallas_call(gather_kernel, out_shape=jax.ShapeDtypeStruct((GROUP, LD,...  3.28 us
    pallas_call x1, Pallas kernels, shards(): pl.pallas_call(spread_kernel, out_shape=jax.ShapeDtypeStruct(rhs_block.sh...  3.23 us
  transfers between devices with their start and end apart: 5, of which 1 were waited for; matrix products, arithmetic and copies ran while one was open for 4% of the time, Pallas kernels for 19%

commit v1 on v0

v1 whole, which is shorter than its diff:
```python
import functools

import jax
import jax.numpy as jnp
from jax import lax
from jax.experimental import pallas as pl
from jax.experimental.pallas import tpu as pltpu
from jax.sharding import Mesh, PartitionSpec as P

F32 = jnp.float32
BF16 = jnp.bfloat16
RANK = 128
LD = 16
TILES = 64
ENT = 192
GROUP = 16
ROWS = 4
TARGETS = 48
LANES = ROWS * RANK
DEPTH = 16


def mm(a, b):
    return jnp.dot(a, b, preferred_element_type=F32)


def mm_nt(a, b):
    return lax.dot_general(a, b, (((1,), (1,)), ((), ())), preferred_element_type=F32)


def gather_kernel(xme, rhs, basis, trans, lists, msg, panels, root):
    x = xme[0]
    current = []
    for g in range(LD):
        panel = mm(rhs[:, g * RANK : (g + 1) * RANK], basis[g * RANK : (g + 1) * RANK, :])
        panels[g * 64 : (g + 1) * 64, :] = panel
        current.append(panel.astype(BF16))
    count = LD
    while count > 1:
        above = []
        for h in range(count // 2):
            pair = jnp.concatenate([current[2 * h], current[2 * h + 1]], axis=1)
            at = count - 2 + 2 * h
            above.append(mm(pair, trans[at : at + 2].reshape(2 * RANK, RANK)))
        current = [a.astype(BF16) for a in above]
        count //= 2
    root[...] = jnp.zeros_like(root)
    root[0:64, :] = above[0]
    slot = lists[0]
    p = slot >> 2
    slot = ((x - (p >> 1)) & 3) * 64 + (p >> 3) * 8 + (p & 1) * 4 + (slot & 3)
    slot = slot.astype(F32).astype(BF16)
    tile = lists[1].astype(F32).astype(BF16)
    none = jnp.full((LD, RANK), -1.0, BF16)
    for j in range(GROUP):
        msg[j, :, 128:256] = none
        msg[j, :, 0:192] = slot
        msg[j, :, 384:512] = none
        msg[j, :, 256:448] = tile
        for r in range(ROWS):
            msg[j, :, 512 + r * RANK : 512 + (r + 1) * RANK] = panels[
                pl.ds(r * GROUP + j, LD, stride=64), :
            ].astype(BF16)
        msg[j, :, 1024:1152] = root[pl.ds(j, 16, stride=16), :].astype(BF16)


def choice_kernel(xme, picks, top, sel, top_counts):
    x = xme[0]
    lane = lax.broadcasted_iota(jnp.int32, (256, 256), 1)
    for t in range(GROUP):
        hot = jnp.where(picks[:, t : t + 1] == lane, 1.0, 0.0).astype(BF16)
        for s in range(4):
            sel[s, t * 64 : (t + 1) * 64, :] = hot[s * 64 : (s + 1) * 64, :]
    n = top[0:1, :]
    source = top[1:2, :]
    tile = top[2:3, :]
    m16 = n - 16
    m32 = n - 32
    m64 = n - 64
    at = jnp.where(
        n >= 16, jnp.where((m16 & 1) == (x >> 1), 12 + (m16 >> 1), -1), n - 4
    )
    at = jnp.where(n >= 32, jnp.where((m32 & 3) == x, 20 + (m32 >> 2), -1), at)
    at = jnp.where(
        n >= 64,
        jnp.where(((m64 >> 1) & 3) == x, 28 + (m64 >> 3) * 2 + (m64 & 1), -1),
        at,
    )
    code = jnp.where(at >= 0, tile * TARGETS + at, -1)
    width = top.shape[1]
    node = lax.broadcasted_iota(jnp.int32, (128, width), 0)
    source_hot = jnp.where(source == node, 1.0, 0.0).astype(BF16)
    part = 8 * TARGETS
    rows = lax.broadcasted_iota(jnp.int32, (part, width), 0)
    for b in range(8):
        hot = jnp.where(code == rows + b * part, 1.0, 0.0).astype(BF16)
        top_counts[b * part : (b + 1) * part, :] = mm_nt(hot, source_hot).astype(BF16)


def tally_kernel(lists, counts, low0, high0, low1, high1):
    one = jnp.ones((), BF16)
    zero = jnp.zeros((), BF16)
    low_ids = lax.broadcasted_iota(jnp.int32, (ENT, 128), 1).astype(F32).astype(BF16)
    high_ids = low_ids + 128
    tile_ids = lax.broadcasted_iota(jnp.int32, (TILES, ENT), 0).astype(F32).astype(BF16)

    def settle(low, high, d, g):
        rows = slice(g * TILES, (g + 1) * TILES)
        counts[d, rows, 0:128] = low[rows, :].astype(BF16)
        counts[d, rows, 128:256] = high[rows, :].astype(BF16)

    def device(d, low, high, low_before, high_before):
        codes = lists[d].astype(F32)
        slots = jnp.transpose(codes[:, 0:256])
        tiles = codes[:, 256 : 256 + ENT]
        for g in range(LD):
            slot = jnp.broadcast_to(slots[0:ENT, g : g + 1], (ENT, 128)).astype(BF16)
            slot_hot = jnp.concatenate(
                [jnp.where(slot == low_ids, one, zero), jnp.where(slot == high_ids, one, zero)],
                axis=1,
            )
            tile = tiles[g : g + 1, :].astype(BF16)
            tally = mm(jnp.where(tile == tile_ids, one, zero), slot_hot)
            low[pl.ds(g, TILES, stride=LD), :] = tally[:, 0:128]
            high[pl.ds(g, TILES, stride=LD), :] = tally[:, 128:256]
            settle(low_before, high_before, jnp.maximum(d - 1, 0), g)

    low1[...] = jnp.zeros_like(low1)
    high1[...] = jnp.zeros_like(high1)

    def two(i, carry):
        device(2 * i, low0, high0, low1, high1)
        device(2 * i + 1, low1, high1, low0, high0)
        return carry

    lax.fori_loop(0, GROUP // 2, two, 0)
    for g in range(LD):
        settle(low1, high1, GROUP - 1, g)


def couple_kernel(
    xme,
    yme,
    a0,
    a1,
    a2,
    a3,
    sel,
    counts,
    top_counts,
    t0,
    t1,
    t2,
    t3,
    tt,
    msg,
    pool,
    zs,
    xtop,
    acc,
    root,
):
    x = xme[0]
    total = 256 + TARGETS
    held = (a0, a1, a2, a3)
    xtop[...] = jnp.zeros_like(xtop)
    acc[...] = jnp.zeros_like(acc)
    root[...] = jnp.zeros_like(root)
    for s in range(4):
        panels = held[s][:, :, 0:LANES].reshape(256, LANES)
        for m in range(4):
            got = mm(sel[s, m * 256 : (m + 1) * 256, :], panels).astype(BF16)
            for t in range(4):
                pool[m * 4 + t, s * 64 : (s + 1) * 64, :] = got[t * 64 : (t + 1) * 64, :]

    def device(d, carry):
        for m in range(4):
            z = mm(counts[d, m * 256 : (m + 1) * 256, :], pool[d]).astype(BF16)
            zs[m * 16 : (m + 1) * 16, d] = z.reshape(16, 16, LANES)
        return carry

    lax.fori_loop(0, GROUP, device, 0)
    for s in range(4):
        for q in range(GROUP):
            n = 64 + (q >> 1) * 8 + ((x - s) & 3) * 2 + (q & 1)
            xtop[pl.ds(n, ROWS, stride=128), :] = held[s][q, :, LANES:].astype(F32)[0:ROWS]
    for n in range(63, 3, -1):
        left = xtop[pl.ds(2 * n, ROWS, stride=128), :]
        right = xtop[pl.ds(2 * n + 1, ROWS, stride=128), :]
        pair = jnp.concatenate([left, right], axis=1).astype(BF16)
        up = mm(pair, tt[2 * n - 8 : 2 * n - 6].reshape(2 * RANK, RANK))
        xtop[pl.ds(n, ROWS, stride=128), :] = up.astype(BF16).astype(F32)
    sources = jnp.concatenate(
        [xtop[r * 128 : (r + 1) * 128, :] for r in range(ROWS)], axis=1
    ).astype(BF16)
    part = 8 * TARGETS
    for b in range(8):
        z = mm(top_counts[b * part : (b + 1) * part, :], sources).astype(BF16)
        zs[b * 8 : (b + 1) * 8, 16:19] = z.reshape(8, 3, 16, LANES)

    for y, table in enumerate((t0, t1, t2, t3)):
        first = ((yme[0] - y) & 3) * 16

        def step(i, carry):
            k = i * DEPTH
            tiles = table[pl.ds(k, DEPTH)].reshape(DEPTH * RANK, RANK)
            for r in range(ROWS):
                lanes = slice(r * RANK, (r + 1) * RANK)
                wide = jnp.concatenate(
                    [zs[first + k + h, :, :, lanes].reshape(total, RANK) for h in range(DEPTH)],
                    axis=1,
                )
                acc[r * total : (r + 1) * total, :] += mm(wide, tiles)
            return carry

        lax.fori_loop(0, 16 // DEPTH, step, 0)

    def get(t):
        return acc[pl.ds(256 + t, ROWS, stride=total), :]

    def add(t, value):
        acc[pl.ds(256 + t, ROWS, stride=total), :] += value

    for i in range(4):
        y = mm_nt(get(i).astype(BF16), tt[2 * i : 2 * i + 2].reshape(2 * RANK, RANK))
        add(4 + 2 * i, y[:, 0:RANK])
        add(5 + 2 * i, y[:, RANK:])
    for z in range(8):
        add(12 + z, mm_nt(get(4 + z).astype(BF16), tt[8 + z * 2 + (x >> 1)]))
    for z in range(8):
        add(20 + z, mm_nt(get(12 + z).astype(BF16), tt[24 + z * 4 + x]))
    for z in range(8):
        pair = tt[pl.ds(56 + z * 8 + x * 2, 2)].reshape(2 * RANK, RANK)
        y = mm_nt(get(20 + z).astype(BF16), pair)
        add(28 + 2 * z, y[:, 0:RANK])
        add(29 + 2 * z, y[:, RANK:])
    for q in range(GROUP):
        for r in range(ROWS):
            msg[q, :, r * RANK : (r + 1) * RANK] = acc[
                r * total + q * 16 : r * total + (q + 1) * 16, :
            ].astype(BF16)
        root[q * 16 : q * 16 + ROWS, :] = get(28 + q)
        msg[q, :, LANES:] = root[q * 16 : (q + 1) * 16, :].astype(BF16)


def spread_kernel(msg, basis, trans, out, panels, root):
    for j in range(GROUP):
        for r in range(ROWS):
            panels[r * 256 + j * 16 : r * 256 + (j + 1) * 16, :] = msg[
                j, :, r * RANK : (r + 1) * RANK
            ].astype(F32)
        root[pl.ds(j, ROWS, stride=GROUP), :] = msg[j, :, LANES:].astype(F32)[0:ROWS]
    current = [root[...]]
    count = 2
    while count <= LD:
        below = []
        for h in range(count // 2):
            at = count - 2 + 2 * h
            y = mm_nt(current[h].astype(BF16), trans[at : at + 2].reshape(2 * RANK, RANK))
            below += [y[:, 0:RANK], y[:, RANK:]]
        current = below
        count *= 2
    for g in range(LD):
        coupled = jnp.concatenate(
            [panels[pl.ds(r * 256 + g, GROUP, stride=16), :] for r in range(ROWS)], axis=0
        )
        w = (current[g] + coupled).astype(BF16)
        out[:, g * RANK : (g + 1) * RANK] = mm_nt(w, basis[g * RANK : (g + 1) * RANK, :]).astype(
            BF16
        )


SMEM = pl.BlockSpec(memory_space=pltpu.SMEM)
WHOLE = pl.BlockSpec(memory_space=pltpu.VMEM)


def params(mib):
    return pltpu.CompilerParams(vmem_limit_bytes=mib * 1024 * 1024)


def cost(flops, moved):
    return pl.CostEstimate(flops=flops, bytes_accessed=moved, transcendentals=0)


def shards(
    rhs_block,
    leaf_basis,
    local_transfer,
    top_transfer,
    coupling_tiles,
    send_index,
    leaf_list,
    top_list,
):
    x = lax.axis_index("x")
    xme = x.astype(jnp.int32).reshape(1)
    trans = local_transfer.reshape(30, RANK, RANK)
    yme = lax.axis_index("rhs").astype(jnp.int32).reshape(1)
    tables = [coupling_tiles] + [
        lax.ppermute(coupling_tiles, "rhs", [(i, (i + s) % 4) for i in range(4)])
        for s in (1, 2, 3)
    ]
    msg = pl.pallas_call(
        gather_kernel,
        out_shape=jax.ShapeDtypeStruct((GROUP, LD, 1152), BF16),
        in_specs=[SMEM] + [WHOLE] * 4,
        out_specs=WHOLE,
        scratch_shapes=[pltpu.VMEM((1024, RANK), F32), pltpu.VMEM((256, RANK), F32)],
        compiler_params=params(60),
        name="leaf_panels",
    )(xme, rhs_block, leaf_basis, trans, leaf_list)
    msg = lax.all_to_all(msg, ("z", "core"), 0, 0, tiled=True)
    mine = msg[:, :, 512:1152]
    blocks = [mine] + [
        lax.ppermute(mine, "x", [(i, (i + s) % 4) for i in range(4)]) for s in (1, 2, 3)
    ]
    index = send_index.reshape(8, 4, 2, 8, 4, 2, 4)
    index = lax.dynamic_index_in_dim(index, x, 4, keepdims=False)
    index = jnp.concatenate(
        [lax.dynamic_slice_in_dim(index, (x - s) % 4, 1, 1) for s in range(4)], axis=1
    )
    index = index.transpose(1, 0, 2, 5, 3, 4)
    place = (jnp.arange(8)[:, None] * 2 + jnp.arange(2)[None, :])[None, :, :, None, None, None]
    picks = jnp.where(index >= 0, index + 16 * place, -1).reshape(256, GROUP).astype(jnp.int32)
    sel, top_counts = pl.pallas_call(
        choice_kernel,
        out_shape=(
            jax.ShapeDtypeStruct((4, 1024, 256), BF16),
            jax.ShapeDtypeStruct((TILES * TARGETS, 128), BF16),
        ),
        in_specs=[SMEM] + [WHOLE] * 2,
        out_specs=(WHOLE, WHOLE),
        compiler_params=params(16),
        cost_estimate=cost(400_000_000, 3_000_000),
        name="choices",
    )(xme, picks, top_list)
    counts = pl.pallas_call(
        tally_kernel,
        out_shape=jax.ShapeDtypeStruct((GROUP, 1024, 256), BF16),
        in_specs=[WHOLE],
        out_specs=WHOLE,
        scratch_shapes=[pltpu.VMEM((1024, 128), F32)] * 4,
        compiler_params=params(6),
        cost_estimate=cost(4_000_000_000, 12_000_000),
        name="tallies",
    )(msg)
    total = 256 + TARGETS
    back = pl.pallas_call(
        couple_kernel,
        out_shape=jax.ShapeDtypeStruct((GROUP, LD, 640), BF16),
        in_specs=[SMEM] * 2 + [WHOLE] * 12,
        out_specs=WHOLE,
        scratch_shapes=[
            pltpu.VMEM((GROUP, 256, LANES), BF16),
            pltpu.VMEM((TILES, 19, 16, LANES), BF16),
            pltpu.VMEM((ROWS * 128, RANK), F32),
            pltpu.VMEM((ROWS * total, RANK), F32),
            pltpu.VMEM((GROUP * 16, RANK), F32),
        ],
        compiler_params=params(28),
        cost_estimate=cost(8_000_000_000, 20_000_000),
        name="interactions",
    )(xme, yme, *blocks, sel, counts, top_counts, *tables, top_transfer)
    back = lax.all_to_all(back, ("z", "core"), 0, 0, tiled=True)
    return pl.pallas_call(
        spread_kernel,
        out_shape=jax.ShapeDtypeStruct(rhs_block.shape, BF16),
        in_specs=[WHOLE] * 3,
        out_specs=WHOLE,
        scratch_shapes=[pltpu.VMEM((1024, RANK), F32), pltpu.VMEM((64, RANK), F32)],
        compiler_params=params(8),
        name="far_field",
    )(back, leaf_basis, trans)


def solution(mesh):
    grid = Mesh(mesh.devices.reshape(8, 4, 2, 4), ("z", "x", "core", "rhs"))
    leaf = ("z", "x", "core")
    placed = (
        P("rhs", leaf),
        P(leaf, None),
        P(leaf, None, None, None),
        P(),
        P("rhs", None, None),
        P(),
        P(None, leaf, None),
        P(),
    )
    return jax.shard_map(
        shards, mesh=grid, in_specs=placed, out_specs=P("rhs", leaf), check_vma=False
    )
```

time: 121 us -> 91.7 us (0.76)
  the two profiles are of different devices: /device:TPU:1 before, /device:TPU:17 now
where the time goes in v1:
time: 91.7 us; the launch traced here: 91.5 us
  Pallas kernels  35.1 us (38%)
  blocking collectives  24.5 us (27%)
  starting transfers between devices  16.4 us (18%)
  local copies, waits for them, and re-layouts  8.36 us (9%)
  waiting for transfers between devices  6.79 us (7%)
    all_to_all x1, blocking collectives, shards(): back = lax.all_to_all(back, ('z', 'core'), 0, 0, tiled=True)  24.5 us
    pallas_call x1, Pallas kernels, shards(): pl.pallas_call(couple_kernel, out_shape=jax.ShapeDtypeStruct((GROUP, LD,...  16 us
    pallas_call x1, Pallas kernels, shards(): pl.pallas_call(tally_kernel, out_shape=jax.ShapeDtypeStruct((GROUP, 1024,...  12.9 us
    all_to_all x1, starting transfers between devices, shards(): msg = lax.all_to_all(msg, ('z', 'core'), 0, 0, tiled=True)  9.15 us
    all_to_all x1, waiting for transfers between devices, shards(): msg = lax.all_to_all(msg, ('z', 'core'), 0, 0, tiled=True)  6.78 us
    ppermute x3, starting transfers between devices, shards(): lax.ppermute(mine, 'x', [(i, (i + s) % 4) for i in range(4)])  4.89 us
    unnamed x21, local copies, waits for them, and re-layouts  4.3 us
    pallas_call x1, Pallas kernels, shards(): pl.pallas_call(gather_kernel, out_shape=jax.ShapeDtypeStruct((GROUP, LD,...  3.33 us
  transfers between devices with their start and end apart: 7, of which 1 were waited for; matrix products, arithmetic and copies ran while one was open for 7% of the time, Pallas kernels for 15%

profile of v1, /device:TPU:17, one launch (start us, length us, event | category | flops | bytes accessed | tf_op | source)
XLA Modules:
  0.0 91.5 jit_solution(5434864106845409247)
XLA Ops:
  0.0 3.3 %leaf_panels.1 = bf16[16,16,1152]{2,1,0:T(8,128)(2,1)} custom-call(s32[1]{0:T(128)} %bitcast.xme, bf16[64,2048]{1,0:T(8,128)(2,1)} %rhs.1, bf16[2048,128]{1,0:T(8,128)(2,1)} %basis.3, bf16[30,128,128]{2,1,0:T(8,128)(2,1)} %bitcast.12, s32[2,16,192]{2,1,0:T(8,128)} %lists.1), custom_call_target="tpu_custom_call" | custom-call | tf_op jit(solution)/shard_map/leaf_panels/pallas_call | solution.py:303
  3.3 9.2 %all-to-all-start = ((bf16[16,16,1152]{2,1,0:T(8,128)(2,1)}), bf16[16,16,1152]{2,1,0:T(8,128)(2,1)S(1)}, u32[]{:S(2)}, u32[]{:S(2)}) async-start(bf16[16,16,1152]{2,1,0:T(8,128)(2,1)} %leaf_panels.1), calls=%async_computation | async-start | bytes 1179648 | tf_op jit(solution)/shard_map/all_to_all | solution.py:312
  12.5 1.1 %collective-permute-start.3 = (bf16[16,128,128]{2,1,0:T(8,128)(2,1)S(1)}, bf16[16,128,128]{2,1,0:T(8,128)(2,1)S(1)}, u32[]{:S(2)}, u32[]{:S(2)}) collective-permute-start(bf16[16,128,128]{2,1,0:T(8,128)(2,1)S(1)} %copy-done.3), channel_id=1, source_target_pairs={{0,1},{1,2},{2,3},{3,0},{4,5},{5,6},{6,7},{7,4},{8,9},{9,10},{10,1... | collective-permute-start | bytes 1572872 | tf_op jit(solution)/shard_map/ppermute | solution.py:300
  13.6 0.4 collective-permute-start.4
  13.9 0.9 collective-permute-start.5
  14.9 2.0 %copy.11 = s32[64,64,4]{2,1,0:T(8,128)} copy(s32[64,64,4]{1,2,0:T(4,128)S(1)} %copy-done.9) | data formatting | bytes 131072 | tf_op args[5]
  16.9 1.1 %constant_dynamic-slice_fusion.3 = (s32[8,1,2,8,1,2,4]{6,5,4,3,2,1,0:T(2,128)S(1)}, s32[8,1,2,8,1,2,4]{6,5,4,3,2,1,0:T(2,128)S(1)}, s32[8,1,2,8,1,2,4]{6,5,4,3,2,1,0:T(2,128)S(1)}, s32[8,1,2,8,1,2,4]{6,5,4,3,2,1,0:T(2,128)S(1)}) fusion(s32[8,4,2,8,4,2,4]{6,5,4,3,2,1,0:T(2,128)} %bitcast.14, s32[]{:T(128)S(6)} %select_n.54, s32[]{:T(128)S(6)} %select_n.56, ...), kind=kLoop, calls=%fused_computation.6 | loop fusion | bytes 32788 | tf_op jit(solution)/shard_map/dynamic_slice | solution.py:320
  18.0 0.3 copy.12
  18.3 0.3 copy.13
  18.6 0.3 copy.14
  18.9 0.3 copy.15
  19.2 0.1 select_bitcast_fusion
  19.3 1.0 %copy.16 = s32[4,8,2,4,8,2]{3,2,1,0,5,4:T(2,128)S(1)} copy(s32[4,8,2,4,8,2]{4,1,3,5,2,0:T(8,128)S(1)} %select_bitcast_fusion) | data formatting | bytes 32768 | tf_op jit(solution)/shard_map/jit(_where)/select_n | solution.py:324
  20.3 0.7 reshape.52
  21.0 0.1 copy.17.picks
  21.1 1.0 %choices.1 = (bf16[4,1024,256]{2,1,0:T(8,128)(2,1)S(1)}, bf16[3072,128]{1,0:T(8,128)(2,1)S(1)}) custom-call(s32[1]{0:T(128)} %bitcast.xme, s32[256,16]{1,0:T(8,128)S(1)} %copy.17.picks, s32[3,512]{1,0:T(4,128)S(1)} %copy-done.4), custom_call_target="tpu_custom_call" | custom-call | flops 400000000 | bytes 3000000 | tf_op jit(solution)/shard_map/choices/pallas_call | solution.py:325
  22.1 1.3 %copy-done.5 = bf16[4,1024,256]{2,1,0:T(8,128)(2,1)} copy-done((bf16[4,1024,256]{2,1,0:T(8,128)(2,1)}, bf16[4,1024,256]{2,1,0:T(8,128)(2,1)S(1)}, u32[]{:S(2)}) %copy-start.5) | copy-done | bytes 2097176
  23.5 0.9 copy-done.7
  24.4 6.8 %all-to-all-done.lists = bf16[16,16,1152]{2,1,0:T(8,128)(2,1)S(1)} async-done(((bf16[16,16,1152]{2,1,0:T(8,128)(2,1)}), bf16[16,16,1152]{2,1,0:T(8,128)(2,1)S(1)}, u32[]{:S(2)}, u32[]{:S(2)}) %all-to-all-start) | async-done | bytes 589856 | tf_op jit(solution)/shard_map/all_to_all | solution.py:312
  31.2 0.0 copy-start.2
  31.2 1.3 %collective-permute-start = (bf16[16,16,640]{2,1,0:T(8,128)(2,1)S(1)}, bf16[16,16,640]{2,1,0:T(8,128)(2,1)S(1)}, u32[]{:S(2)}, u32[]{:S(2)}) collective-permute-start(bf16[16,16,640]{2,1,0:T(8,128)(2,1)S(1)} %slice.4.a0), channel_id=1, source_target_pairs={{0,8},{8,16},{16,24},{24,0},{1,9},{9,17},{17,25},{25,1},{2,10},{10... | collective-permute-start | bytes 983048 | tf_op jit(solution)/shard_map/ppermute | solution.py:315
  32.5 2.4 %collective-permute-start.1 = (bf16[16,16,640]{2,1,0:T(8,128)(2,1)S(1)}, bf16[16,16,640]{2,1,0:T(8,128)(2,1)S(1)}, u32[]{:S(2)}, u32[]{:S(2)}) collective-permute-start(bf16[16,16,640]{2,1,0:T(8,128)(2,1)S(1)} %slice.4.a0), channel_id=1, source_target_pairs={{0,16},{8,24},{16,0},{24,8},{1,17},{9,25},{17,1},{25,9},{2,18},{10... | collective-permute-start | bytes 983048 | tf_op jit(solution)/shard_map/ppermute | solution.py:315
  35.0 0.0 collective-permute-done.3.t1
  35.0 1.2 %collective-permute-start.2 = (bf16[16,16,640]{2,1,0:T(8,128)(2,1)S(1)}, bf16[16,16,640]{2,1,0:T(8,128)(2,1)S(1)}, u32[]{:S(2)}, u32[]{:S(2)}) collective-permute-start(bf16[16,16,640]{2,1,0:T(8,128)(2,1)S(1)} %slice.4.a0), channel_id=1, source_target_pairs={{0,24},{8,0},{16,8},{24,16},{1,25},{9,1},{17,9},{25,17},{2,26},{10... | collective-permute-start | bytes 983048 | tf_op jit(solution)/shard_map/ppermute | solution.py:315
  36.1 12.9 %tallies.1.counts = bf16[16,1024,256]{2,1,0:T(8,128)(2,1)S(1)} custom-call(bf16[16,16,1152]{2,1,0:T(8,128)(2,1)S(1)} %all-to-all-done.lists), custom_call_target="tpu_custom_call" | custom-call | flops 4000000000 | bytes 12000000 | tf_op jit(solution)/shard_map/tallies/pallas_call | solution.py:337
  49.0 0.0 collective-permute-done.4.t2
  49.0 0.0 collective-permute-done.a1
  49.1 0.0 copy-start
  49.1 0.0 copy-start.1
  49.1 16.0 %interactions.1 = bf16[16,16,640]{2,1,0:T(8,128)(2,1)S(1)} custom-call(s32[1]{0:T(128)} %bitcast.xme, s32[1]{0:T(128)} %bitcast.1.yme, bf16[16,16,640]{2,1,0:T(8,128)(2,1)S(1)} %slice.4.a0, bf16[16,16,640]{2,1,0:T(8,128)(2,1)S(1)} %collective-permute-done.a1, bf16[16,16,640]{2,1,0:T(8,128)(2,1)S(1)} %collective-permute-done.1.a2, ...), custom_call_target="tpu_custom_call" | custom-call | flops 8000000000 | bytes 20000000 | tf_op jit(solution)/shard_map/interactions/pallas_call | solution.py:348
  65.2 24.5 %all_to_all.10.msg = bf16[16,16,640]{2,1,0:T(8,128)(2,1)S(1)} all-to-all(bf16[16,16,640]{2,1,0:T(8,128)(2,1)S(1)} %interactions.1), channel_id=1, replica_groups=mesh['z'=8,'x'=4,'core'=2,'rhs'=4] {'z','core'}, dimensions={0} | all-to-all | bytes 655360 | tf_op jit(solution)/shard_map/all_to_all | solution.py:364
  89.7 1.8 %far_field.1 = bf16[64,2048]{1,0:T(8,128)(2,1)} custom-call(bf16[16,16,640]{2,1,0:T(8,128)(2,1)S(1)} %all_to_all.10.msg, bf16[2048,128]{1,0:T(8,128)(2,1)S(1)} %copy-done.1, bf16[30,128,128]{2,1,0:T(8,128)(2,1)S(1)} %bitcast.13), custom_call_target="tpu_custom_call" | custom-call | tf_op jit(solution)/shard_map/far_field/pallas_call | solution.py:365
  (21 shorter events, 0.1 us)
Async XLA Ops:
  0.0 12.5 %copy-start.3 = (bf16[16,128,128]{2,1,0:T(8,128)(2,1)S(1)}, bf16[16,128,128]{2,1,0:T(8,128)(2,1)}, u32[]{:S(2)}) copy-start(bf16[16,128,128]{2,1,0:T(8,128)(2,1)} %t0.1) | copy-start | bytes 1572868
  0.0 14.9 %copy-start.9 = (s32[64,64,4]{1,2,0:T(4,128)S(1)}, s32[64,64,4]{1,2,0:T(4,128)}, u32[]{:S(2)}) copy-start(s32[64,64,4]{1,2,0:T(4,128)} %param.13) | copy-start | bytes 196612
  3.3 27.8 %all-to-all-start = ((bf16[16,16,1152]{2,1,0:T(8,128)(2,1)}), bf16[16,16,1152]{2,1,0:T(8,128)(2,1)S(1)}, u32[]{:S(2)}, u32[]{:S(2)}) async-start(bf16[16,16,1152]{2,1,0:T(8,128)(2,1)} %leaf_panels.1), calls=%async_computation | async-start | bytes 1179648 | tf_op jit(solution)/shard_map/all_to_all | solution.py:312
  12.5 22.5 %collective-permute-start.3 = (bf16[16,128,128]{2,1,0:T(8,128)(2,1)S(1)}, bf16[16,128,128]{2,1,0:T(8,128)(2,1)S(1)}, u32[]{:S(2)}, u32[]{:S(2)}) collective-permute-start(bf16[16,128,128]{2,1,0:T(8,128)(2,1)S(1)} %copy-done.3), channel_id=1, source_target_pairs={{0,1},{1,2},{2,3},{3,0},{4,5},{5,6},{6,7},{7,4},{8,9},{9,10},{10,1... | collective-permute-start | bytes 1572872 | tf_op jit(solution)/shard_map/ppermute | solution.py:300
  13.6 35.4 %collective-permute-start.4 = (bf16[16,128,128]{2,1,0:T(8,128)(2,1)S(1)}, bf16[16,128,128]{2,1,0:T(8,128)(2,1)S(1)}, u32[]{:S(2)}, u32[]{:S(2)}) collective-permute-start(bf16[16,128,128]{2,1,0:T(8,128)(2,1)S(1)} %copy-done.3), channel_id=1, source_target_pairs={{0,2},{1,3},{2,0},{3,1},{4,6},{5,7},{6,4},{7,5},{8,10},{9,11},{10,... | collective-permute-start | bytes 1572872 | tf_op jit(solution)/shard_map/ppermute | solution.py:300
  13.9 35.1 %collective-permute-start.5 = (bf16[16,128,128]{2,1,0:T(8,128)(2,1)S(1)}, bf16[16,128,128]{2,1,0:T(8,128)(2,1)S(1)}, u32[]{:S(2)}, u32[]{:S(2)}) collective-permute-start(bf16[16,128,128]{2,1,0:T(8,128)(2,1)S(1)} %copy-done.3), channel_id=1, source_target_pairs={{0,3},{1,0},{2,1},{3,2},{4,7},{5,4},{6,5},{7,6},{8,11},{9,8},{10,9... | collective-permute-start | bytes 1572872 | tf_op jit(solution)/shard_map/ppermute | solution.py:300
  16.9 4.2 %copy-start.4 = (s32[3,512]{1,0:T(4,128)S(1)}, s32[3,512]{1,0:T(4,128)}, u32[]{:S(2)}) copy-start(s32[3,512]{1,0:T(4,128)} %top.1) | copy-start | bytes 18436
  22.1 1.3 %copy-start.5 = (bf16[4,1024,256]{2,1,0:T(8,128)(2,1)}, bf16[4,1024,256]{2,1,0:T(8,128)(2,1)S(1)}, u32[]{:S(2)}) copy-start(bf16[4,1024,256]{2,1,0:T(8,128)(2,1)S(1)} %get-tuple-element.7.sel) | copy-start | bytes 6291460
  23.5 0.9 copy-start.7
  31.2 17.9 %copy-start.2 = (bf16[120,128,128]{2,1,0:T(8,128)(2,1)S(1)}, bf16[120,128,128]{2,1,0:T(8,128)(2,1)}, u32[]{:S(2)}) copy-start(bf16[120,128,128]{2,1,0:T(8,128)(2,1)} %tt.1) | copy-start | bytes 11796484
  31.2 17.9 %copy-start.6 = (bf16[4,1024,256]{2,1,0:T(8,128)(2,1)S(1)}, bf16[4,1024,256]{2,1,0:T(8,128)(2,1)}, u32[]{:S(2)}) copy-start(bf16[4,1024,256]{2,1,0:T(8,128)(2,1)} %copy-done.5) | copy-start | bytes 6291460
  31.2 17.9 %copy-start.8 = (bf16[3072,128]{1,0:T(8,128)(2,1)S(1)}, bf16[3072,128]{1,0:T(8,128)(2,1)}, u32[]{:S(2)}) copy-start(bf16[3072,128]{1,0:T(8,128)(2,1)} %copy-done.7) | copy-start | bytes 2359300
  31.2 17.8 %collective-permute-start = (bf16[16,16,640]{2,1,0:T(8,128)(2,1)S(1)}, bf16[16,16,640]{2,1,0:T(8,128)(2,1)S(1)}, u32[]{:S(2)}, u32[]{:S(2)}) collective-permute-start(bf16[16,16,640]{2,1,0:T(8,128)(2,1)S(1)} %slice.4.a0), channel_id=1, source_target_pairs={{0,8},{8,16},{16,24},{24,0},{1,9},{9,17},{17,25},{25,1},{2,10},{10... | collective-permute-start | bytes 983048 | tf_op jit(solution)/shard_map/ppermute | solution.py:315
  32.5 16.5 %collective-permute-start.1 = (bf16[16,16,640]{2,1,0:T(8,128)(2,1)S(1)}, bf16[16,16,640]{2,1,0:T(8,128)(2,1)S(1)}, u32[]{:S(2)}, u32[]{:S(2)}) collective-permute-start(bf16[16,16,640]{2,1,0:T(8,128)(2,1)S(1)} %slice.4.a0), channel_id=1, source_target_pairs={{0,16},{8,24},{16,0},{24,8},{1,17},{9,25},{17,1},{25,9},{2,18},{10... | collective-permute-start | bytes 983048 | tf_op jit(solution)/shard_map/ppermute | solution.py:315
  35.0 14.1 %collective-permute-start.2 = (bf16[16,16,640]{2,1,0:T(8,128)(2,1)S(1)}, bf16[16,16,640]{2,1,0:T(8,128)(2,1)S(1)}, u32[]{:S(2)}, u32[]{:S(2)}) collective-permute-start(bf16[16,16,640]{2,1,0:T(8,128)(2,1)S(1)} %slice.4.a0), channel_id=1, source_target_pairs={{0,24},{8,0},{16,8},{24,16},{1,25},{9,1},{17,9},{25,17},{2,26},{10... | collective-permute-start | bytes 983048 | tf_op jit(solution)/shard_map/ppermute | solution.py:315
  49.1 40.6 %copy-start = (bf16[1,30,128,128]{3,2,1,0:T(8,128)(2,1)S(1)}, bf16[1,30,128,128]{3,2,1,0:T(8,128)(2,1)}, u32[]{:S(2)}) copy-start(bf16[1,30,128,128]{3,2,1,0:T(8,128)(2,1)} %param.10) | copy-start | bytes 2949124
  49.1 40.6 %copy-start.1 = (bf16[2048,128]{1,0:T(8,128)(2,1)S(1)}, bf16[2048,128]{1,0:T(8,128)(2,1)}, u32[]{:S(2)}) copy-start(bf16[2048,128]{1,0:T(8,128)(2,1)} %basis.3) | copy-start | bytes 1572868

commit v2 on v1

--- a/solution.py
+++ b/solution.py
@@ -17,6 +17,7 @@
 ROWS = 4
 TARGETS = 48
 LANES = ROWS * RANK
+CHUNK = 32
 DEPTH = 16
 
 
@@ -49,24 +50,38 @@
     slot = lists[0]
     p = slot >> 2
     slot = ((x - (p >> 1)) & 3) * 64 + (p >> 3) * 8 + (p & 1) * 4 + (slot & 3)
-    slot = slot.astype(F32).astype(BF16)
-    tile = lists[1].astype(F32).astype(BF16)
-    none = jnp.full((LD, RANK), -1.0, BF16)
+    slot = slot.astype(F32)
+    tile = lists[1].astype(F32)
+    codes = jnp.concatenate([slot, tile], axis=1).astype(BF16)
     for j in range(GROUP):
-        msg[j, :, 128:256] = none
-        msg[j, :, 0:192] = slot
-        msg[j, :, 384:512] = none
-        msg[j, :, 256:448] = tile
+        msg[j, :, 0 : 2 * ENT] = codes
+        msg[j, :, 384:512] = root[pl.ds(j, 16, stride=16), :].astype(BF16)
         for r in range(ROWS):
             msg[j, :, 512 + r * RANK : 512 + (r + 1) * RANK] = panels[
                 pl.ds(r * GROUP + j, LD, stride=64), :
             ].astype(BF16)
-        msg[j, :, 1024:1152] = root[pl.ds(j, 16, stride=16), :].astype(BF16)
-
-
-def choice_kernel(xme, picks, top, sel, top_counts):
+
+
+def pack_kernel(msg, out, root):
+    out[0:256, :] = msg[:, :, 512:1024].reshape(256, LANES)
+    root[...] = msg[:, :, 384:512].reshape(256, RANK).astype(F32)
+    for r in range(ROWS):
+        out[256:272, r * RANK : (r + 1) * RANK] = root[pl.ds(r, GROUP, stride=LD), :].astype(BF16)
+
+
+def choice_kernel(xme, index, top, sel, top_counts, rows):
     x = xme[0]
-    lane = lax.broadcasted_iota(jnp.int32, (256, 256), 1)
+    for s in range(4):
+        for q in range(GROUP):
+            p = (q >> 1) * 8 + ((x - s) & 3) * 2 + (q & 1)
+            rows[s * 64 + q * 4 : s * 64 + q * 4 + 4, :] = index[p].astype(F32)
+    d = lax.broadcasted_iota(jnp.int32, (64, GROUP), 0)
+    t = lax.broadcasted_iota(jnp.int32, (64, GROUP), 1)
+    mine = jnp.where(d == (t >> 1) * 8 + x * 2 + (t & 1), 1.0, 0.0).astype(BF16)
+    picks = mm(rows[...].astype(BF16), mine)
+    place = lax.broadcasted_iota(jnp.int32, (256, GROUP), 0)
+    picks = jnp.where(picks >= 0, picks + ((place >> 2) & 15).astype(F32) * 16, -1.0)
+    lane = lax.broadcasted_iota(jnp.int32, (256, 256), 1).astype(F32)
     for t in range(GROUP):
         hot = jnp.where(picks[:, t : t + 1] == lane, 1.0, 0.0).astype(BF16)
         for s in range(4):
@@ -112,7 +127,7 @@
     def device(d, low, high, low_before, high_before):
         codes = lists[d].astype(F32)
         slots = jnp.transpose(codes[:, 0:256])
-        tiles = codes[:, 256 : 256 + ENT]
+        tiles = codes[:, ENT : 2 * ENT]
         for g in range(LD):
             slot = jnp.broadcast_to(slots[0:ENT, g : g + 1], (ENT, 128)).astype(BF16)
             slot_hot = jnp.concatenate(
@@ -165,25 +180,25 @@
     held = (a0, a1, a2, a3)
     xtop[...] = jnp.zeros_like(xtop)
     acc[...] = jnp.zeros_like(acc)
-    root[...] = jnp.zeros_like(root)
     for s in range(4):
-        panels = held[s][:, :, 0:LANES].reshape(256, LANES)
-        for m in range(4):
-            got = mm(sel[s, m * 256 : (m + 1) * 256, :], panels).astype(BF16)
-            for t in range(4):
-                pool[m * 4 + t, s * 64 : (s + 1) * 64, :] = got[t * 64 : (t + 1) * 64, :]
+        panels = held[s][0:256, :]
+        got = mm(sel[s], panels).astype(BF16)
+        for t in range(GROUP):
+            pool[t, s * 64 : (s + 1) * 64, :] = got[t * 64 : (t + 1) * 64, :]
 
     def device(d, carry):
-        for m in range(4):
-            z = mm(counts[d, m * 256 : (m + 1) * 256, :], pool[d]).astype(BF16)
-            zs[m * 16 : (m + 1) * 16, d] = z.reshape(16, 16, LANES)
+        for m in range(TILES // CHUNK):
+            z = mm(counts[d, m * CHUNK * 16 : (m + 1) * CHUNK * 16, :], pool[d]).astype(BF16)
+            zs[m * CHUNK : (m + 1) * CHUNK, d] = z.reshape(CHUNK, 16, LANES)
         return carry
 
     lax.fori_loop(0, GROUP, device, 0)
     for s in range(4):
-        for q in range(GROUP):
-            n = 64 + (q >> 1) * 8 + ((x - s) & 3) * 2 + (q & 1)
-            xtop[pl.ds(n, ROWS, stride=128), :] = held[s][q, :, LANES:].astype(F32)[0:ROWS]
+        for r in range(ROWS):
+            root[0:GROUP, :] = held[s][256:272, r * RANK : (r + 1) * RANK].astype(F32)
+            for z in range(8):
+                n = 64 + z * 8 + ((x - s) & 3) * 2
+                xtop[pl.ds(r * 128 + n, 2), :] = root[2 * z : 2 * z + 2, :]
     for n in range(63, 3, -1):
         left = xtop[pl.ds(2 * n, ROWS, stride=128), :]
         right = xtop[pl.ds(2 * n + 1, ROWS, stride=128), :]
@@ -234,6 +249,7 @@
         y = mm_nt(get(20 + z).astype(BF16), pair)
         add(28 + 2 * z, y[:, 0:RANK])
         add(29 + 2 * z, y[:, RANK:])
+    root[...] = jnp.zeros_like(root)
     for q in range(GROUP):
         for r in range(ROWS):
             msg[q, :, r * RANK : (r + 1) * RANK] = acc[
@@ -302,7 +318,7 @@
     ]
     msg = pl.pallas_call(
         gather_kernel,
-        out_shape=jax.ShapeDtypeStruct((GROUP, LD, 1152), BF16),
+        out_shape=jax.ShapeDtypeStruct((GROUP, LD, 1024), BF16),
         in_specs=[SMEM] + [WHOLE] * 4,
         out_specs=WHOLE,
         scratch_shapes=[pltpu.VMEM((1024, RANK), F32), pltpu.VMEM((256, RANK), F32)],
@@ -310,18 +326,18 @@
         name="leaf_panels",
     )(xme, rhs_block, leaf_basis, trans, leaf_list)
     msg = lax.all_to_all(msg, ("z", "core"), 0, 0, tiled=True)
-    mine = msg[:, :, 512:1152]
+    mine = pl.pallas_call(
+        pack_kernel,
+        out_shape=jax.ShapeDtypeStruct((272, LANES), BF16),
+        in_specs=[WHOLE],
+        out_specs=WHOLE,
+        scratch_shapes=[pltpu.VMEM((256, RANK), F32)],
+        compiler_params=params(4),
+        name="pack",
+    )(msg)
     blocks = [mine] + [
         lax.ppermute(mine, "x", [(i, (i + s) % 4) for i in range(4)]) for s in (1, 2, 3)
     ]
-    index = send_index.reshape(8, 4, 2, 8, 4, 2, 4)
-    index = lax.dynamic_index_in_dim(index, x, 4, keepdims=False)
-    index = jnp.concatenate(
-        [lax.dynamic_slice_in_dim(index, (x - s) % 4, 1, 1) for s in range(4)], axis=1
-    )
-    index = index.transpose(1, 0, 2, 5, 3, 4)
-    place = (jnp.arange(8)[:, None] * 2 + jnp.arange(2)[None, :])[None, :, :, None, None, None]
-    picks = jnp.where(index >= 0, index + 16 * place, -1).reshape(256, GROUP).astype(jnp.int32)
     sel, top_counts = pl.pallas_call(
         choice_kernel,
         out_shape=(
@@ -330,10 +346,11 @@
         ),
         in_specs=[SMEM] + [WHOLE] * 2,
         out_specs=(WHOLE, WHOLE),
-        compiler_params=params(16),
+        scratch_shapes=[pltpu.VMEM((256, 64), F32)],
+        compiler_params=params(56),
         cost_estimate=cost(400_000_000, 3_000_000),
         name="choices",
-    )(xme, picks, top_list)
+    )(xme, send_index.transpose(0, 2, 1), top_list)
     counts = pl.pallas_call(
         tally_kernel,
         out_shape=jax.ShapeDtypeStruct((GROUP, 1024, 256), BF16),

time: 91.7 us -> 92 us (level)
  local copies, waits for them, and re-layouts: 8.36 us -> 0.03 us
  waiting for transfers between devices: 6.79 us -> 11.7 us
  Pallas kernels: 35.1 us -> 37.6 us
  blocking collectives: 24.5 us -> 26 us
    all_to_all x1, waiting for transfers between devices: 6.78 us -> 11.6 us  [shards(): msg = lax.all_to_all(msg, ('z', 'core'), 0, 0, tiled=True)]
    unnamed x21 -> x12, local copies, waits for them, and re-layouts: 4.3 us -> 0.03 us
    pallas_call x1, Pallas kernels: 1.03 us -> 3.39 us  [shards(): pl.pallas_call(choice_kernel, out_shape=(jax.ShapeDtypeStruct((4, 1024, 2...]
    dynamic_slice x5 -> x0, local copies, waits for them, and re-layouts: 2.24 us -> none  [shards(): lax.dynamic_slice_in_dim(index, (x - s) % 4, 1, 1)]
    all_to_all x1, blocking collectives: 24.5 us -> 26 us  [shards(): back = lax.all_to_all(back, ('z', 'core'), 0, 0, tiled=True)]
    select_n x1 -> x0, local copies, waits for them, and re-layouts: 1.01 us -> none  [shards(): jnp.where(index >= 0, index + 16 * place, -1).reshape(256, GROUP)]
  transfers between devices with their start and end apart: 7 -> 7, of which waited for: 1 -> 1; matrix products, arithmetic and copies ran while one was open for 7% -> 0% of each run, Pallas kernels for 15% -> 18%
where the time goes in v2:
time: 92 us; the launch traced here: 91.8 us
  Pallas kernels  37.6 us (41%)
  blocking collectives  26 us (28%)
  starting transfers between devices  16.3 us (18%)
  waiting for transfers between devices  11.7 us (13%)
    all_to_all x1, blocking collectives, shards(): back = lax.all_to_all(back, ('z', 'core'), 0, 0, tiled=True)  26 us
    pallas_call x1, Pallas kernels, shards(): pl.pallas_call(couple_kernel, out_shape=jax.ShapeDtypeStruct((GROUP, LD,...  16.1 us
    pallas_call x1, Pallas kernels, shards(): pl.pallas_call(tally_kernel, out_shape=jax.ShapeDtypeStruct((GROUP, 1024,...  13.1 us
    all_to_all x1, waiting for transfers between devices, shards(): msg = lax.all_to_all(msg, ('z', 'core'), 0, 0, tiled=True)  11.6 us
    all_to_all x1, starting transfers between devices, shards(): msg = lax.all_to_all(msg, ('z', 'core'), 0, 0, tiled=True)  9.15 us
    ppermute x3, starting transfers between devices, shards(): lax.ppermute(mine, 'x', [(i, (i + s) % 4) for i in range(4)])  4.89 us
    pallas_call x1, Pallas kernels, shards(): pl.pallas_call(choice_kernel, out_shape=(jax.ShapeDtypeStruct((4, 1024, 2...  3.39 us
    pallas_call x1, Pallas kernels, shards(): pl.pallas_call(gather_kernel, out_shape=jax.ShapeDtypeStruct((GROUP, LD,...  3.26 us
  transfers between devices with their start and end apart: 7, of which 1 were waited for; matrix products, arithmetic and copies ran while one was open for 0% of the time, Pallas kernels for 18%

profile of v2, /device:TPU:17, one launch (start us, length us, event | category | flops | bytes accessed | tf_op | source)
XLA Modules:
  0.0 91.8 jit_solution(3100353346065586380)
XLA Ops:
  0.0 3.3 %leaf_panels.1 = bf16[16,16,1024]{2,1,0:T(8,128)(2,1)} custom-call(s32[1]{0:T(128)} %bitcast.xme, bf16[64,2048]{1,0:T(8,128)(2,1)} %rhs.1, bf16[2048,128]{1,0:T(8,128)(2,1)} %basis.3, bf16[30,128,128]{2,1,0:T(8,128)(2,1)} %bitcast.4, s32[2,16,192]{2,1,0:T(8,128)} %lists.1), custom_call_target="tpu_custom_call" | custom-call | tf_op jit(solution)/shard_map/leaf_panels/pallas_call | solution.py:319
  3.3 9.2 %all-to-all-start = ((bf16[16,16,1024]{2,1,0:T(8,128)(2,1)}), bf16[16,16,1024]{2,1,0:T(8,128)(2,1)S(1)}, u32[]{:S(2)}, u32[]{:S(2)}) async-start(bf16[16,16,1024]{2,1,0:T(8,128)(2,1)} %leaf_panels.1), calls=%async_computation | async-start | bytes 1048576 | tf_op jit(solution)/shard_map/all_to_all | solution.py:328
  12.4 1.0 %collective-permute-start.3 = (bf16[16,128,128]{2,1,0:T(8,128)(2,1)}, bf16[16,128,128]{2,1,0:T(8,128)(2,1)S(1)}, u32[]{:S(2)}, u32[]{:S(2)}) collective-permute-start(bf16[16,128,128]{2,1,0:T(8,128)(2,1)} %t0.1), channel_id=1, source_target_pairs={{0,1},{1,2},{2,3},{3,0},{4,5},{5,6},{6,7},{7,4},{8,9},{9,10},{10,1... | collective-permute-start | bytes 1572872 | tf_op jit(solution)/shard_map/ppermute | solution.py:316
  13.4 0.3 collective-permute-start.4
  13.8 0.9 %collective-permute-start.5 = (bf16[16,128,128]{2,1,0:T(8,128)(2,1)}, bf16[16,128,128]{2,1,0:T(8,128)(2,1)S(1)}, u32[]{:S(2)}, u32[]{:S(2)}) collective-permute-start(bf16[16,128,128]{2,1,0:T(8,128)(2,1)} %t0.1), channel_id=1, source_target_pairs={{0,3},{1,0},{2,1},{3,2},{4,7},{5,4},{6,5},{7,6},{8,11},{9,8},{10,9... | collective-permute-start | bytes 1572872 | tf_op jit(solution)/shard_map/ppermute | solution.py:316
  14.7 3.4 %choices.1 = (bf16[4,1024,256]{2,1,0:T(8,128)(2,1)}, bf16[3072,128]{1,0:T(8,128)(2,1)}) custom-call(s32[1]{0:T(128)} %bitcast.xme, s32[64,4,64]{2,1,0:T(4,128)} %bitcast.6, s32[3,512]{1,0:T(4,128)} %top.1), custom_call_target="tpu_custom_call" | custom-call | flops 400000000 | bytes 3000000 | tf_op jit(solution)/shard_map/choices/pallas_call | solution.py:341
  18.1 11.6 %all-to-all-done.msg.lists = bf16[16,16,1024]{2,1,0:T(8,128)(2,1)S(1)} async-done(((bf16[16,16,1024]{2,1,0:T(8,128)(2,1)}), bf16[16,16,1024]{2,1,0:T(8,128)(2,1)S(1)}, u32[]{:S(2)}, u32[]{:S(2)}) %all-to-all-start) | async-done | bytes 524320 | tf_op jit(solution)/shard_map/all_to_all | solution.py:328
  29.8 0.0 copy-start.2
  29.8 0.0 copy-start.3
  29.8 0.0 copy-start.4
  29.8 0.0 copy-start.5
  29.8 1.3 %collective-permute-start = (bf16[272,512]{1,0:T(8,128)(2,1)S(1)}, bf16[272,512]{1,0:T(8,128)(2,1)S(1)}, u32[]{:S(2)}, u32[]{:S(2)}) collective-permute-start(bf16[272,512]{1,0:T(8,128)(2,1)S(1)} %pack.1.a0), channel_id=1, source_target_pairs={{0,8},{8,16},{16,24},{24,0},{1,9},{9,17},{17,25},{25,1},{2,10},{10... | collective-permute-start | bytes 835592 | tf_op jit(solution)/shard_map/ppermute | solution.py:339
  31.1 2.5 %collective-permute-start.1 = (bf16[272,512]{1,0:T(8,128)(2,1)S(1)}, bf16[272,512]{1,0:T(8,128)(2,1)S(1)}, u32[]{:S(2)}, u32[]{:S(2)}) collective-permute-start(bf16[272,512]{1,0:T(8,128)(2,1)S(1)} %pack.1.a0), channel_id=1, source_target_pairs={{0,16},{8,24},{16,0},{24,8},{1,17},{9,25},{17,1},{25,9},{2,18},{10... | collective-permute-start | bytes 835592 | tf_op jit(solution)/shard_map/ppermute | solution.py:339
  33.6 0.0 collective-permute-done.3.t1
  33.6 1.2 %collective-permute-start.2 = (bf16[272,512]{1,0:T(8,128)(2,1)S(1)}, bf16[272,512]{1,0:T(8,128)(2,1)S(1)}, u32[]{:S(2)}, u32[]{:S(2)}) collective-permute-start(bf16[272,512]{1,0:T(8,128)(2,1)S(1)} %pack.1.a0), channel_id=1, source_target_pairs={{0,24},{8,0},{16,8},{24,16},{1,25},{9,1},{17,9},{25,17},{2,26},{10... | collective-permute-start | bytes 835592 | tf_op jit(solution)/shard_map/ppermute | solution.py:339
  34.7 13.1 %tallies.1.counts = bf16[16,1024,256]{2,1,0:T(8,128)(2,1)S(1)} custom-call(bf16[16,16,1024]{2,1,0:T(8,128)(2,1)S(1)} %all-to-all-done.msg.lists), custom_call_target="tpu_custom_call" | custom-call | flops 4000000000 | bytes 12000000 | tf_op jit(solution)/shard_map/tallies/pallas_call | solution.py:354
  47.8 0.0 collective-permute-done.4.t2
  47.8 0.0 collective-permute-done.5.t3
  47.8 0.0 collective-permute-done.a1
  47.9 0.0 collective-permute-done.1.a2
  47.9 0.0 collective-permute-done.2.a3
  47.9 0.0 copy-done.2
  47.9 0.0 copy-done.3
  47.9 0.0 copy-done.4
  47.9 0.0 copy-done.5
  47.9 0.0 copy-start
  47.9 0.0 copy-start.1
  47.9 16.1 %interactions.1 = bf16[16,16,640]{2,1,0:T(8,128)(2,1)S(1)} custom-call(s32[1]{0:T(128)} %bitcast.xme, s32[1]{0:T(128)} %bitcast.1.yme, bf16[272,512]{1,0:T(8,128)(2,1)S(1)} %pack.1.a0, bf16[272,512]{1,0:T(8,128)(2,1)S(1)} %collective-permute-done.a1, bf16[272,512]{1,0:T(8,128)(2,1)S(1)} %collective-permute-done.1.a2, ...), custom_call_target="tpu_custom_call" | custom-call | flops 8000000000 | bytes 20000000 | tf_op jit(solution)/shard_map/interactions/pallas_call | solution.py:365
  64.0 26.0 %all_to_all.10.msg = bf16[16,16,640]{2,1,0:T(8,128)(2,1)S(1)} all-to-all(bf16[16,16,640]{2,1,0:T(8,128)(2,1)S(1)} %interactions.1), channel_id=1, replica_groups=mesh['z'=8,'x'=4,'core'=2,'rhs'=4] {'z','core'}, dimensions={0} | all-to-all | bytes 655360 | tf_op jit(solution)/shard_map/all_to_all | solution.py:381
  90.0 0.0 copy-done
  90.0 0.0 copy-done.1
  90.0 1.8 %far_field.1 = bf16[64,2048]{1,0:T(8,128)(2,1)} custom-call(bf16[16,16,640]{2,1,0:T(8,128)(2,1)S(1)} %all_to_all.10.msg, bf16[2048,128]{1,0:T(8,128)(2,1)S(1)} %copy-done.1, bf16[30,128,128]{2,1,0:T(8,128)(2,1)S(1)} %bitcast.5), custom_call_target="tpu_custom_call" | custom-call | tf_op jit(solution)/shard_map/far_field/pallas_call | solution.py:382
  (1 shorter events, 0.0 us)
Async XLA Ops:
  3.3 26.5 %all-to-all-start = ((bf16[16,16,1024]{2,1,0:T(8,128)(2,1)}), bf16[16,16,1024]{2,1,0:T(8,128)(2,1)S(1)}, u32[]{:S(2)}, u32[]{:S(2)}) async-start(bf16[16,16,1024]{2,1,0:T(8,128)(2,1)} %leaf_panels.1), calls=%async_computation | async-start | bytes 1048576 | tf_op jit(solution)/shard_map/all_to_all | solution.py:328
  12.4 21.2 %collective-permute-start.3 = (bf16[16,128,128]{2,1,0:T(8,128)(2,1)}, bf16[16,128,128]{2,1,0:T(8,128)(2,1)S(1)}, u32[]{:S(2)}, u32[]{:S(2)}) collective-permute-start(bf16[16,128,128]{2,1,0:T(8,128)(2,1)} %t0.1), channel_id=1, source_target_pairs={{0,1},{1,2},{2,3},{3,0},{4,5},{5,6},{6,7},{7,4},{8,9},{9,10},{10,1... | collective-permute-start | bytes 1572872 | tf_op jit(solution)/shard_map/ppermute | solution.py:316
  13.4 34.4 %collective-permute-start.4 = (bf16[16,128,128]{2,1,0:T(8,128)(2,1)}, bf16[16,128,128]{2,1,0:T(8,128)(2,1)S(1)}, u32[]{:S(2)}, u32[]{:S(2)}) collective-permute-start(bf16[16,128,128]{2,1,0:T(8,128)(2,1)} %t0.1), channel_id=1, source_target_pairs={{0,2},{1,3},{2,0},{3,1},{4,6},{5,7},{6,4},{7,5},{8,10},{9,11},{10,... | collective-permute-start | bytes 1572872 | tf_op jit(solution)/shard_map/ppermute | solution.py:316
  13.8 34.1 %collective-permute-start.5 = (bf16[16,128,128]{2,1,0:T(8,128)(2,1)}, bf16[16,128,128]{2,1,0:T(8,128)(2,1)S(1)}, u32[]{:S(2)}, u32[]{:S(2)}) collective-permute-start(bf16[16,128,128]{2,1,0:T(8,128)(2,1)} %t0.1), channel_id=1, source_target_pairs={{0,3},{1,0},{2,1},{3,2},{4,7},{5,4},{6,5},{7,6},{8,11},{9,8},{10,9... | collective-permute-start | bytes 1572872 | tf_op jit(solution)/shard_map/ppermute | solution.py:316
  29.8 18.1 %copy-start.2 = (bf16[120,128,128]{2,1,0:T(8,128)(2,1)S(1)}, bf16[120,128,128]{2,1,0:T(8,128)(2,1)}, u32[]{:S(2)}) copy-start(bf16[120,128,128]{2,1,0:T(8,128)(2,1)} %tt.1) | copy-start | bytes 11796484
  29.8 18.1 %copy-start.3 = (bf16[16,128,128]{2,1,0:T(8,128)(2,1)S(1)}, bf16[16,128,128]{2,1,0:T(8,128)(2,1)}, u32[]{:S(2)}) copy-start(bf16[16,128,128]{2,1,0:T(8,128)(2,1)} %t0.1) | copy-start | bytes 1572868
  29.8 18.1 %copy-start.4 = (bf16[4,1024,256]{2,1,0:T(8,128)(2,1)S(1)}, bf16[4,1024,256]{2,1,0:T(8,128)(2,1)}, u32[]{:S(2)}) copy-start(bf16[4,1024,256]{2,1,0:T(8,128)(2,1)} %get-tuple-element.7.sel) | copy-start | bytes 6291460
  29.8 18.1 %copy-start.5 = (bf16[3072,128]{1,0:T(8,128)(2,1)S(1)}, bf16[3072,128]{1,0:T(8,128)(2,1)}, u32[]{:S(2)}) copy-start(bf16[3072,128]{1,0:T(8,128)(2,1)} %get-tuple-element.8.top_counts) | copy-start | bytes 2359300
  29.8 18.0 %collective-permute-start = (bf16[272,512]{1,0:T(8,128)(2,1)S(1)}, bf16[272,512]{1,0:T(8,128)(2,1)S(1)}, u32[]{:S(2)}, u32[]{:S(2)}) collective-permute-start(bf16[272,512]{1,0:T(8,128)(2,1)S(1)} %pack.1.a0), channel_id=1, source_target_pairs={{0,8},{8,16},{16,24},{24,0},{1,9},{9,17},{17,25},{25,1},{2,10},{10... | collective-permute-start | bytes 835592 | tf_op jit(solution)/shard_map/ppermute | solution.py:339
  31.1 16.7 %collective-permute-start.1 = (bf16[272,512]{1,0:T(8,128)(2,1)S(1)}, bf16[272,512]{1,0:T(8,128)(2,1)S(1)}, u32[]{:S(2)}, u32[]{:S(2)}) collective-permute-start(bf16[272,512]{1,0:T(8,128)(2,1)S(1)} %pack.1.a0), channel_id=1, source_target_pairs={{0,16},{8,24},{16,0},{24,8},{1,17},{9,25},{17,1},{25,9},{2,18},{10... | collective-permute-start | bytes 835592 | tf_op jit(solution)/shard_map/ppermute | solution.py:339
  33.6 14.3 %collective-permute-start.2 = (bf16[272,512]{1,0:T(8,128)(2,1)S(1)}, bf16[272,512]{1,0:T(8,128)(2,1)S(1)}, u32[]{:S(2)}, u32[]{:S(2)}) collective-permute-start(bf16[272,512]{1,0:T(8,128)(2,1)S(1)} %pack.1.a0), channel_id=1, source_target_pairs={{0,24},{8,0},{16,8},{24,16},{1,25},{9,1},{17,9},{25,17},{2,26},{10... | collective-permute-start | bytes 835592 | tf_op jit(solution)/shard_map/ppermute | solution.py:339
  47.9 42.1 %copy-start = (bf16[1,30,128,128]{3,2,1,0:T(8,128)(2,1)S(1)}, bf16[1,30,128,128]{3,2,1,0:T(8,128)(2,1)}, u32[]{:S(2)}) copy-start(bf16[1,30,128,128]{3,2,1,0:T(8,128)(2,1)} %param.10) | copy-start | bytes 2949124
  47.9 42.1 %copy-start.1 = (bf16[2048,128]{1,0:T(8,128)(2,1)S(1)}, bf16[2048,128]{1,0:T(8,128)(2,1)}, u32[]{:S(2)}) copy-start(bf16[2048,128]{1,0:T(8,128)(2,1)} %basis.3) | copy-start | bytes 1572868

commit v3 on v2

--- a/solution.py
+++ b/solution.py
@@ -214,7 +214,7 @@
         zs[b * 8 : (b + 1) * 8, 16:19] = z.reshape(8, 3, 16, LANES)
 
     for y, table in enumerate((t0, t1, t2, t3)):
-        first = ((yme[0] - y) & 3) * 16
+        first = (yme[0] ^ y) * 16
 
         def step(i, carry):
             k = i * DEPTH
@@ -312,10 +312,8 @@
     xme = x.astype(jnp.int32).reshape(1)
     trans = local_transfer.reshape(30, RANK, RANK)
     yme = lax.axis_index("rhs").astype(jnp.int32).reshape(1)
-    tables = [coupling_tiles] + [
-        lax.ppermute(coupling_tiles, "rhs", [(i, (i + s) % 4) for i in range(4)])
-        for s in (1, 2, 3)
-    ]
+    near = lax.ppermute(coupling_tiles, "rhs", [(i, i ^ 1) for i in range(4)])
+    over = lax.ppermute(coupling_tiles, "rhs", [(i, i ^ 3) for i in range(4)])
     msg = pl.pallas_call(
         gather_kernel,
         out_shape=jax.ShapeDtypeStruct((GROUP, LD, 1024), BF16),
@@ -351,6 +349,9 @@
         cost_estimate=cost(400_000_000, 3_000_000),
         name="choices",
     )(xme, send_index.transpose(0, 2, 1), top_list)
+    near, top_counts = lax.optimization_barrier((near, top_counts))
+    across = lax.ppermute(near, "rhs", [(i, i ^ 3) for i in range(4)])
+    tables = (coupling_tiles, near, across, over)
     counts = pl.pallas_call(
         tally_kernel,
         out_shape=jax.ShapeDtypeStruct((GROUP, 1024, 256), BF16),

time: 92 us -> 87.7 us (0.953)
  the two profiles are of different devices: /device:TPU:17 before, /device:TPU:1 now
where the time goes in v3:
time: 87.7 us; the launch traced here: 87.5 us
  Pallas kernels  37.7 us (43%)
  starting transfers between devices  20.8 us (24%)
  blocking collectives  20.8 us (24%)
  waiting for transfers between devices  8.01 us (9%)
    all_to_all x1, blocking collectives, shards(): back = lax.all_to_all(back, ('z', 'core'), 0, 0, tiled=True)  20.8 us
    pallas_call x1, Pallas kernels, shards(): pl.pallas_call(couple_kernel, out_shape=jax.ShapeDtypeStruct((GROUP, LD,...  16.1 us
    pallas_call x1, Pallas kernels, shards(): pl.pallas_call(tally_kernel, out_shape=jax.ShapeDtypeStruct((GROUP, 1024,...  13.1 us
    all_to_all x1, starting transfers between devices, shards(): msg = lax.all_to_all(msg, ('z', 'core'), 0, 0, tiled=True)  9.98 us
    ppermute x1, waiting for transfers between devices, shards(): near = lax.ppermute(coupling_tiles, 'rhs', [(i, i ^ 1) for i in range(4)])  6.97 us
    ppermute x3, starting transfers between devices, shards(): lax.ppermute(mine, 'x', [(i, (i + s) % 4) for i in range(4)])  4.9 us
    pallas_call x1, Pallas kernels, shards(): pl.pallas_call(choice_kernel, out_shape=(jax.ShapeDtypeStruct((4, 1024, 2...  3.38 us
    pallas_call x1, Pallas kernels, shards(): pl.pallas_call(gather_kernel, out_shape=jax.ShapeDtypeStruct((GROUP, LD,...  3.26 us
  transfers between devices with their start and end apart: 7, of which 2 were waited for; matrix products, arithmetic and copies ran while one was open for 0% of the time, Pallas kernels for 19%

profile of v3, /device:TPU:1, one launch (start us, length us, event | category | flops | bytes accessed | tf_op | source)
XLA Modules:
  0.0 87.5 jit_solution(4987689804442032457)
XLA Ops:
  0.0 3.3 %leaf_panels.1 = bf16[16,16,1024]{2,1,0:T(8,128)(2,1)} custom-call(s32[1]{0:T(128)} %bitcast.xme, bf16[64,2048]{1,0:T(8,128)(2,1)} %rhs.1, bf16[2048,128]{1,0:T(8,128)(2,1)} %basis.3, bf16[30,128,128]{2,1,0:T(8,128)(2,1)} %bitcast.4, s32[2,16,192]{2,1,0:T(8,128)} %lists.1), custom_call_target="tpu_custom_call" | custom-call | tf_op jit(solution)/shard_map/leaf_panels/pallas_call | solution.py:317
  3.3 10.0 %all-to-all-start = ((bf16[16,16,1024]{2,1,0:T(8,128)(2,1)}), bf16[16,16,1024]{2,1,0:T(8,128)(2,1)S(1)}, u32[]{:S(2)}, u32[]{:S(2)}) async-start(bf16[16,16,1024]{2,1,0:T(8,128)(2,1)} %leaf_panels.1), calls=%async_computation | async-start | bytes 1048576 | tf_op jit(solution)/shard_map/all_to_all | solution.py:326
  13.2 1.3 %collective-permute-start.3 = (bf16[16,128,128]{2,1,0:T(8,128)(2,1)}, bf16[16,128,128]{2,1,0:T(8,128)(2,1)S(1)}, u32[]{:S(2)}, u32[]{:S(2)}) collective-permute-start(bf16[16,128,128]{2,1,0:T(8,128)(2,1)} %t0.1), channel_id=1, source_target_pairs={{0,1},{1,0},{2,3},{3,2},{4,5},{5,4},{6,7},{7,6},{8,9},{9,8},{10,11... | collective-permute-start | bytes 1572872 | tf_op jit(solution)/shard_map/ppermute | solution.py:315
  14.5 1.9 %collective-permute-start.5 = (bf16[16,128,128]{2,1,0:T(8,128)(2,1)}, bf16[16,128,128]{2,1,0:T(8,128)(2,1)S(1)}, u32[]{:S(2)}, u32[]{:S(2)}) collective-permute-start(bf16[16,128,128]{2,1,0:T(8,128)(2,1)} %t0.1), channel_id=1, source_target_pairs={{0,3},{1,2},{2,1},{3,0},{4,7},{5,6},{6,5},{7,4},{8,11},{9,10},{10,... | collective-permute-start | bytes 1572872 | tf_op jit(solution)/shard_map/ppermute | solution.py:316
  16.4 3.4 %choices.1 = (bf16[4,1024,256]{2,1,0:T(8,128)(2,1)}, bf16[3072,128]{1,0:T(8,128)(2,1)}) custom-call(s32[1]{0:T(128)} %bitcast.xme, s32[64,4,64]{2,1,0:T(4,128)} %bitcast.6, s32[3,512]{1,0:T(4,128)} %top.1), custom_call_target="tpu_custom_call" | custom-call | flops 400000000 | bytes 3000000 | tf_op jit(solution)/shard_map/choices/pallas_call | solution.py:339
  19.8 7.0 %collective-permute-done.3.t1 = bf16[16,128,128]{2,1,0:T(8,128)(2,1)S(1)} collective-permute-done((bf16[16,128,128]{2,1,0:T(8,128)(2,1)}, bf16[16,128,128]{2,1,0:T(8,128)(2,1)S(1)}, u32[]{:S(2)}, u32[]{:S(2)}) %collective-permute-start.3) | collective-permute-done | bytes 524320 | tf_op jit(solution)/shard_map/ppermute | solution.py:315
  26.8 2.7 %collective-permute-start.4 = (bf16[16,128,128]{2,1,0:T(8,128)(2,1)S(1)}, bf16[16,128,128]{2,1,0:T(8,128)(2,1)S(1)}, u32[]{:S(2)}, u32[]{:S(2)}) collective-permute-start(bf16[16,128,128]{2,1,0:T(8,128)(2,1)S(1)} %collective-permute-done.3.t1), channel_id=1, source_target_pairs={{0,3},{1,2},{2,1},{3,0},{4,7},{5,6},{6,5},{7,4},{8,11},{9,10},{10,... | collective-permute-start | bytes 1572872 | tf_op jit(solution)/shard_map/ppermute | solution.py:353
  29.5 1.0 %all-to-all-done.msg.lists = bf16[16,16,1024]{2,1,0:T(8,128)(2,1)S(1)} async-done(((bf16[16,16,1024]{2,1,0:T(8,128)(2,1)}), bf16[16,16,1024]{2,1,0:T(8,128)(2,1)S(1)}, u32[]{:S(2)}, u32[]{:S(2)}) %all-to-all-start) | async-done | bytes 524320 | tf_op jit(solution)/shard_map/all_to_all | solution.py:326
  30.6 0.0 copy-start.2
  30.6 0.0 copy-start.3
  30.6 0.0 copy-start.4
  30.6 0.0 copy-start.5
  30.7 1.3 %collective-permute-start = (bf16[272,512]{1,0:T(8,128)(2,1)S(1)}, bf16[272,512]{1,0:T(8,128)(2,1)S(1)}, u32[]{:S(2)}, u32[]{:S(2)}) collective-permute-start(bf16[272,512]{1,0:T(8,128)(2,1)S(1)} %pack.1.a0), channel_id=1, source_target_pairs={{0,8},{8,16},{16,24},{24,0},{1,9},{9,17},{17,25},{25,1},{2,10},{10... | collective-permute-start | bytes 835592 | tf_op jit(solution)/shard_map/ppermute | solution.py:337
  31.9 2.5 %collective-permute-start.1 = (bf16[272,512]{1,0:T(8,128)(2,1)S(1)}, bf16[272,512]{1,0:T(8,128)(2,1)S(1)}, u32[]{:S(2)}, u32[]{:S(2)}) collective-permute-start(bf16[272,512]{1,0:T(8,128)(2,1)S(1)} %pack.1.a0), channel_id=1, source_target_pairs={{0,16},{8,24},{16,0},{24,8},{1,17},{9,25},{17,1},{25,9},{2,18},{10... | collective-permute-start | bytes 835592 | tf_op jit(solution)/shard_map/ppermute | solution.py:337
  34.4 1.2 %collective-permute-start.2 = (bf16[272,512]{1,0:T(8,128)(2,1)S(1)}, bf16[272,512]{1,0:T(8,128)(2,1)S(1)}, u32[]{:S(2)}, u32[]{:S(2)}) collective-permute-start(bf16[272,512]{1,0:T(8,128)(2,1)S(1)} %pack.1.a0), channel_id=1, source_target_pairs={{0,24},{8,0},{16,8},{24,16},{1,25},{9,1},{17,9},{25,17},{2,26},{10... | collective-permute-start | bytes 835592 | tf_op jit(solution)/shard_map/ppermute | solution.py:337
  35.5 13.1 %tallies.1.counts = bf16[16,1024,256]{2,1,0:T(8,128)(2,1)S(1)} custom-call(bf16[16,16,1024]{2,1,0:T(8,128)(2,1)S(1)} %all-to-all-done.msg.lists), custom_call_target="tpu_custom_call" | custom-call | flops 4000000000 | bytes 12000000 | tf_op jit(solution)/shard_map/tallies/pallas_call | solution.py:355
  48.6 0.0 collective-permute-done.5.t3
  48.7 0.0 collective-permute-done.4.t2
  48.7 0.0 collective-permute-done.a1
  48.7 0.0 collective-permute-done.1.a2
  48.7 0.0 collective-permute-done.2.a3
  48.7 0.0 copy-done.2
  48.7 0.0 copy-done.3
  48.7 0.0 copy-done.4
  48.7 0.0 copy-done.5
  48.7 0.0 copy-start
  48.8 0.0 copy-start.1
  48.8 16.1 %interactions.1 = bf16[16,16,640]{2,1,0:T(8,128)(2,1)S(1)} custom-call(s32[1]{0:T(128)} %bitcast.xme, s32[1]{0:T(128)} %bitcast.1.yme, bf16[272,512]{1,0:T(8,128)(2,1)S(1)} %pack.1.a0, bf16[272,512]{1,0:T(8,128)(2,1)S(1)} %collective-permute-done.a1, bf16[272,512]{1,0:T(8,128)(2,1)S(1)} %collective-permute-done.1.a2, ...), custom_call_target="tpu_custom_call" | custom-call | flops 8000000000 | bytes 20000000 | tf_op jit(solution)/shard_map/interactions/pallas_call | solution.py:366
  64.9 20.8 %all_to_all.10.msg = bf16[16,16,640]{2,1,0:T(8,128)(2,1)S(1)} all-to-all(bf16[16,16,640]{2,1,0:T(8,128)(2,1)S(1)} %interactions.1), channel_id=1, replica_groups=mesh['z'=8,'x'=4,'core'=2,'rhs'=4] {'z','core'}, dimensions={0} | all-to-all | bytes 655360 | tf_op jit(solution)/shard_map/all_to_all | solution.py:382
  85.7 0.0 copy-done
  85.7 0.0 copy-done.1
  85.7 1.8 %far_field.1 = bf16[64,2048]{1,0:T(8,128)(2,1)} custom-call(bf16[16,16,640]{2,1,0:T(8,128)(2,1)S(1)} %all_to_all.10.msg, bf16[2048,128]{1,0:T(8,128)(2,1)S(1)} %copy-done.1, bf16[30,128,128]{2,1,0:T(8,128)(2,1)S(1)} %bitcast.5), custom_call_target="tpu_custom_call" | custom-call | tf_op jit(solution)/shard_map/far_field/pallas_call | solution.py:383
  (1 shorter events, 0.0 us)
Async XLA Ops:
  3.3 27.3 %all-to-all-start = ((bf16[16,16,1024]{2,1,0:T(8,128)(2,1)}), bf16[16,16,1024]{2,1,0:T(8,128)(2,1)S(1)}, u32[]{:S(2)}, u32[]{:S(2)}) async-start(bf16[16,16,1024]{2,1,0:T(8,128)(2,1)} %leaf_panels.1), calls=%async_computation | async-start | bytes 1048576 | tf_op jit(solution)/shard_map/all_to_all | solution.py:326
  13.2 13.6 %collective-permute-start.3 = (bf16[16,128,128]{2,1,0:T(8,128)(2,1)}, bf16[16,128,128]{2,1,0:T(8,128)(2,1)S(1)}, u32[]{:S(2)}, u32[]{:S(2)}) collective-permute-start(bf16[16,128,128]{2,1,0:T(8,128)(2,1)} %t0.1), channel_id=1, source_target_pairs={{0,1},{1,0},{2,3},{3,2},{4,5},{5,4},{6,7},{7,6},{8,9},{9,8},{10,11... | collective-permute-start | bytes 1572872 | tf_op jit(solution)/shard_map/ppermute | solution.py:315
  14.5 34.1 %collective-permute-start.5 = (bf16[16,128,128]{2,1,0:T(8,128)(2,1)}, bf16[16,128,128]{2,1,0:T(8,128)(2,1)S(1)}, u32[]{:S(2)}, u32[]{:S(2)}) collective-permute-start(bf16[16,128,128]{2,1,0:T(8,128)(2,1)} %t0.1), channel_id=1, source_target_pairs={{0,3},{1,2},{2,1},{3,0},{4,7},{5,6},{6,5},{7,4},{8,11},{9,10},{10,... | collective-permute-start | bytes 1572872 | tf_op jit(solution)/shard_map/ppermute | solution.py:316
  26.8 21.9 %collective-permute-start.4 = (bf16[16,128,128]{2,1,0:T(8,128)(2,1)S(1)}, bf16[16,128,128]{2,1,0:T(8,128)(2,1)S(1)}, u32[]{:S(2)}, u32[]{:S(2)}) collective-permute-start(bf16[16,128,128]{2,1,0:T(8,128)(2,1)S(1)} %collective-permute-done.3.t1), channel_id=1, source_target_pairs={{0,3},{1,2},{2,1},{3,0},{4,7},{5,6},{6,5},{7,4},{8,11},{9,10},{10,... | collective-permute-start | bytes 1572872 | tf_op jit(solution)/shard_map/ppermute | solution.py:353
  30.6 18.1 %copy-start.2 = (bf16[120,128,128]{2,1,0:T(8,128)(2,1)S(1)}, bf16[120,128,128]{2,1,0:T(8,128)(2,1)}, u32[]{:S(2)}) copy-start(bf16[120,128,128]{2,1,0:T(8,128)(2,1)} %tt.1) | copy-start | bytes 11796484
  30.6 18.1 %copy-start.3 = (bf16[16,128,128]{2,1,0:T(8,128)(2,1)S(1)}, bf16[16,128,128]{2,1,0:T(8,128)(2,1)}, u32[]{:S(2)}) copy-start(bf16[16,128,128]{2,1,0:T(8,128)(2,1)} %t0.1) | copy-start | bytes 1572868
  30.6 18.1 %copy-start.4 = (bf16[4,1024,256]{2,1,0:T(8,128)(2,1)S(1)}, bf16[4,1024,256]{2,1,0:T(8,128)(2,1)}, u32[]{:S(2)}) copy-start(bf16[4,1024,256]{2,1,0:T(8,128)(2,1)} %get-tuple-element.9.sel) | copy-start | bytes 6291460
  30.6 18.1 %copy-start.5 = (bf16[3072,128]{1,0:T(8,128)(2,1)S(1)}, bf16[3072,128]{1,0:T(8,128)(2,1)}, u32[]{:S(2)}) copy-start(bf16[3072,128]{1,0:T(8,128)(2,1)} %get-tuple-element.11.top_counts) | copy-start | bytes 2359300
  30.7 18.0 %collective-permute-start = (bf16[272,512]{1,0:T(8,128)(2,1)S(1)}, bf16[272,512]{1,0:T(8,128)(2,1)S(1)}, u32[]{:S(2)}, u32[]{:S(2)}) collective-permute-start(bf16[272,512]{1,0:T(8,128)(2,1)S(1)} %pack.1.a0), channel_id=1, source_target_pairs={{0,8},{8,16},{16,24},{24,0},{1,9},{9,17},{17,25},{25,1},{2,10},{10... | collective-permute-start | bytes 835592 | tf_op jit(solution)/shard_map/ppermute | solution.py:337
  31.9 16.7 %collective-permute-start.1 = (bf16[272,512]{1,0:T(8,128)(2,1)S(1)}, bf16[272,512]{1,0:T(8,128)(2,1)S(1)}, u32[]{:S(2)}, u32[]{:S(2)}) collective-permute-start(bf16[272,512]{1,0:T(8,128)(2,1)S(1)} %pack.1.a0), channel_id=1, source_target_pairs={{0,16},{8,24},{16,0},{24,8},{1,17},{9,25},{17,1},{25,9},{2,18},{10... | collective-permute-start | bytes 835592 | tf_op jit(solution)/shard_map/ppermute | solution.py:337
  34.4 14.3 %collective-permute-start.2 = (bf16[272,512]{1,0:T(8,128)(2,1)S(1)}, bf16[272,512]{1,0:T(8,128)(2,1)S(1)}, u32[]{:S(2)}, u32[]{:S(2)}) collective-permute-start(bf16[272,512]{1,0:T(8,128)(2,1)S(1)} %pack.1.a0), channel_id=1, source_target_pairs={{0,24},{8,0},{16,8},{24,16},{1,25},{9,1},{17,9},{25,17},{2,26},{10... | collective-permute-start | bytes 835592 | tf_op jit(solution)/shard_map/ppermute | solution.py:337
  48.7 37.0 %copy-start = (bf16[1,30,128,128]{3,2,1,0:T(8,128)(2,1)S(1)}, bf16[1,30,128,128]{3,2,1,0:T(8,128)(2,1)}, u32[]{:S(2)}) copy-start(bf16[1,30,128,128]{3,2,1,0:T(8,128)(2,1)} %param.10) | copy-start | bytes 2949124
  48.8 37.0 %copy-start.1 = (bf16[2048,128]{1,0:T(8,128)(2,1)S(1)}, bf16[2048,128]{1,0:T(8,128)(2,1)}, u32[]{:S(2)}) copy-start(bf16[2048,128]{1,0:T(8,128)(2,1)} %basis.3) | copy-start | bytes 1572868

commit v4 on v3

--- a/solution.py
+++ b/solution.py
@@ -192,7 +192,7 @@
             zs[m * CHUNK : (m + 1) * CHUNK, d] = z.reshape(CHUNK, 16, LANES)
         return carry
 
-    lax.fori_loop(0, GROUP, device, 0)
+    lax.fori_loop(0, GROUP, device, 0, unroll=2)
     for s in range(4):
         for r in range(ROWS):
             root[0:GROUP, :] = held[s][256:272, r * RANK : (r + 1) * RANK].astype(F32)

time: 87.7 us -> 86.4 us (0.985)
  Pallas kernels: 37.7 us -> 36.4 us
    pallas_call x1, Pallas kernels: 16.1 us -> 14.8 us  [shards(): pl.pallas_call(couple_kernel, out_shape=jax.ShapeDtypeStruct((GROUP, LD,...]
where the time goes in v4:
time: 86.4 us; the launch traced here: 86.2 us
  Pallas kernels  36.4 us (42%)
  starting transfers between devices  20.8 us (24%)
  blocking collectives  20.8 us (24%)
  waiting for transfers between devices  8.01 us (9%)
    all_to_all x1, blocking collectives, shards(): back = lax.all_to_all(back, ('z', 'core'), 0, 0, tiled=True)  20.8 us
    pallas_call x1, Pallas kernels, shards(): pl.pallas_call(couple_kernel, out_shape=jax.ShapeDtypeStruct((GROUP, LD,...  14.8 us
    pallas_call x1, Pallas kernels, shards(): pl.pallas_call(tally_kernel, out_shape=jax.ShapeDtypeStruct((GROUP, 1024,...  13.1 us
    all_to_all x1, starting transfers between devices, shards(): msg = lax.all_to_all(msg, ('z', 'core'), 0, 0, tiled=True)  9.98 us
    ppermute x1, waiting for transfers between devices, shards(): near = lax.ppermute(coupling_tiles, 'rhs', [(i, i ^ 1) for i in range(4)])  6.97 us
    ppermute x3, starting transfers between devices, shards(): lax.ppermute(mine, 'x', [(i, (i + s) % 4) for i in range(4)])  4.9 us
    pallas_call x1, Pallas kernels, shards(): pl.pallas_call(choice_kernel, out_shape=(jax.ShapeDtypeStruct((4, 1024, 2...  3.38 us
    pallas_call x1, Pallas kernels, shards(): pl.pallas_call(gather_kernel, out_shape=jax.ShapeDtypeStruct((GROUP, LD,...  3.26 us
  transfers between devices with their start and end apart: 7, of which 2 were waited for; matrix products, arithmetic and copies ran while one was open for 0% of the time, Pallas kernels for 19%

profile of v4, /device:TPU:1, one launch (start us, length us, event | category | flops | bytes accessed | tf_op | source)
XLA Modules:
  0.0 86.2 jit_solution(13960665851761809295)
XLA Ops:
  0.0 3.3 %leaf_panels.1 = bf16[16,16,1024]{2,1,0:T(8,128)(2,1)} custom-call(s32[1]{0:T(128)} %bitcast.xme, bf16[64,2048]{1,0:T(8,128)(2,1)} %rhs.1, bf16[2048,128]{1,0:T(8,128)(2,1)} %basis.3, bf16[30,128,128]{2,1,0:T(8,128)(2,1)} %bitcast.4, s32[2,16,192]{2,1,0:T(8,128)} %lists.1), custom_call_target="tpu_custom_call" | custom-call | tf_op jit(solution)/shard_map/leaf_panels/pallas_call | solution.py:317
  3.3 10.0 %all-to-all-start = ((bf16[16,16,1024]{2,1,0:T(8,128)(2,1)}), bf16[16,16,1024]{2,1,0:T(8,128)(2,1)S(1)}, u32[]{:S(2)}, u32[]{:S(2)}) async-start(bf16[16,16,1024]{2,1,0:T(8,128)(2,1)} %leaf_panels.1), calls=%async_computation | async-start | bytes 1048576 | tf_op jit(solution)/shard_map/all_to_all | solution.py:326
  13.2 1.3 %collective-permute-start.3 = (bf16[16,128,128]{2,1,0:T(8,128)(2,1)}, bf16[16,128,128]{2,1,0:T(8,128)(2,1)S(1)}, u32[]{:S(2)}, u32[]{:S(2)}) collective-permute-start(bf16[16,128,128]{2,1,0:T(8,128)(2,1)} %t0.1), channel_id=1, source_target_pairs={{0,1},{1,0},{2,3},{3,2},{4,5},{5,4},{6,7},{7,6},{8,9},{9,8},{10,11... | collective-permute-start | bytes 1572872 | tf_op jit(solution)/shard_map/ppermute | solution.py:315
  14.5 1.9 %collective-permute-start.5 = (bf16[16,128,128]{2,1,0:T(8,128)(2,1)}, bf16[16,128,128]{2,1,0:T(8,128)(2,1)S(1)}, u32[]{:S(2)}, u32[]{:S(2)}) collective-permute-start(bf16[16,128,128]{2,1,0:T(8,128)(2,1)} %t0.1), channel_id=1, source_target_pairs={{0,3},{1,2},{2,1},{3,0},{4,7},{5,6},{6,5},{7,4},{8,11},{9,10},{10,... | collective-permute-start | bytes 1572872 | tf_op jit(solution)/shard_map/ppermute | solution.py:316
  16.4 3.4 %choices.1 = (bf16[4,1024,256]{2,1,0:T(8,128)(2,1)}, bf16[3072,128]{1,0:T(8,128)(2,1)}) custom-call(s32[1]{0:T(128)} %bitcast.xme, s32[64,4,64]{2,1,0:T(4,128)} %bitcast.6, s32[3,512]{1,0:T(4,128)} %top.1), custom_call_target="tpu_custom_call" | custom-call | flops 400000000 | bytes 3000000 | tf_op jit(solution)/shard_map/choices/pallas_call | solution.py:339
  19.8 7.0 %collective-permute-done.3.t1 = bf16[16,128,128]{2,1,0:T(8,128)(2,1)S(1)} collective-permute-done((bf16[16,128,128]{2,1,0:T(8,128)(2,1)}, bf16[16,128,128]{2,1,0:T(8,128)(2,1)S(1)}, u32[]{:S(2)}, u32[]{:S(2)}) %collective-permute-start.3) | collective-permute-done | bytes 524320 | tf_op jit(solution)/shard_map/ppermute | solution.py:315
  26.8 2.7 %collective-permute-start.4 = (bf16[16,128,128]{2,1,0:T(8,128)(2,1)S(1)}, bf16[16,128,128]{2,1,0:T(8,128)(2,1)S(1)}, u32[]{:S(2)}, u32[]{:S(2)}) collective-permute-start(bf16[16,128,128]{2,1,0:T(8,128)(2,1)S(1)} %collective-permute-done.3.t1), channel_id=1, source_target_pairs={{0,3},{1,2},{2,1},{3,0},{4,7},{5,6},{6,5},{7,4},{8,11},{9,10},{10,... | collective-permute-start | bytes 1572872 | tf_op jit(solution)/shard_map/ppermute | solution.py:353
  29.5 1.0 %all-to-all-done.msg.lists = bf16[16,16,1024]{2,1,0:T(8,128)(2,1)S(1)} async-done(((bf16[16,16,1024]{2,1,0:T(8,128)(2,1)}), bf16[16,16,1024]{2,1,0:T(8,128)(2,1)S(1)}, u32[]{:S(2)}, u32[]{:S(2)}) %all-to-all-start) | async-done | bytes 524320 | tf_op jit(solution)/shard_map/all_to_all | solution.py:326
  30.6 0.0 copy-start.2
  30.6 0.0 copy-start.3
  30.6 0.0 copy-start.4
  30.6 0.0 copy-start.5
  30.7 1.3 %collective-permute-start = (bf16[272,512]{1,0:T(8,128)(2,1)S(1)}, bf16[272,512]{1,0:T(8,128)(2,1)S(1)}, u32[]{:S(2)}, u32[]{:S(2)}) collective-permute-start(bf16[272,512]{1,0:T(8,128)(2,1)S(1)} %pack.1.a0), channel_id=1, source_target_pairs={{0,8},{8,16},{16,24},{24,0},{1,9},{9,17},{17,25},{25,1},{2,10},{10... | collective-permute-start | bytes 835592 | tf_op jit(solution)/shard_map/ppermute | solution.py:337
  31.9 2.5 %collective-permute-start.1 = (bf16[272,512]{1,0:T(8,128)(2,1)S(1)}, bf16[272,512]{1,0:T(8,128)(2,1)S(1)}, u32[]{:S(2)}, u32[]{:S(2)}) collective-permute-start(bf16[272,512]{1,0:T(8,128)(2,1)S(1)} %pack.1.a0), channel_id=1, source_target_pairs={{0,16},{8,24},{16,0},{24,8},{1,17},{9,25},{17,1},{25,9},{2,18},{10... | collective-permute-start | bytes 835592 | tf_op jit(solution)/shard_map/ppermute | solution.py:337
  34.4 1.2 %collective-permute-start.2 = (bf16[272,512]{1,0:T(8,128)(2,1)S(1)}, bf16[272,512]{1,0:T(8,128)(2,1)S(1)}, u32[]{:S(2)}, u32[]{:S(2)}) collective-permute-start(bf16[272,512]{1,0:T(8,128)(2,1)S(1)} %pack.1.a0), channel_id=1, source_target_pairs={{0,24},{8,0},{16,8},{24,16},{1,25},{9,1},{17,9},{25,17},{2,26},{10... | collective-permute-start | bytes 835592 | tf_op jit(solution)/shard_map/ppermute | solution.py:337
  35.5 13.1 %tallies.1.counts = bf16[16,1024,256]{2,1,0:T(8,128)(2,1)S(1)} custom-call(bf16[16,16,1024]{2,1,0:T(8,128)(2,1)S(1)} %all-to-all-done.msg.lists), custom_call_target="tpu_custom_call" | custom-call | flops 4000000000 | bytes 12000000 | tf_op jit(solution)/shard_map/tallies/pallas_call | solution.py:355
  48.6 0.0 collective-permute-done.5.t3
  48.7 0.0 collective-permute-done.4.t2
  48.7 0.0 collective-permute-done.a1
  48.7 0.0 collective-permute-done.1.a2
  48.7 0.0 collective-permute-done.2.a3
  48.7 0.0 copy-done.2
  48.7 0.0 copy-done.3
  48.7 0.0 copy-done.4
  48.7 0.0 copy-done.5
  48.7 0.0 copy-start
  48.8 0.0 copy-start.1
  48.8 14.8 %interactions.1 = bf16[16,16,640]{2,1,0:T(8,128)(2,1)S(1)} custom-call(s32[1]{0:T(128)} %bitcast.xme, s32[1]{0:T(128)} %bitcast.1.yme, bf16[272,512]{1,0:T(8,128)(2,1)S(1)} %pack.1.a0, bf16[272,512]{1,0:T(8,128)(2,1)S(1)} %collective-permute-done.a1, bf16[272,512]{1,0:T(8,128)(2,1)S(1)} %collective-permute-done.1.a2, ...), custom_call_target="tpu_custom_call" | custom-call | flops 8000000000 | bytes 20000000 | tf_op jit(solution)/shard_map/interactions/pallas_call | solution.py:366
  63.6 20.8 %all_to_all.10.msg = bf16[16,16,640]{2,1,0:T(8,128)(2,1)S(1)} all-to-all(bf16[16,16,640]{2,1,0:T(8,128)(2,1)S(1)} %interactions.1), channel_id=1, replica_groups=mesh['z'=8,'x'=4,'core'=2,'rhs'=4] {'z','core'}, dimensions={0} | all-to-all | bytes 655360 | tf_op jit(solution)/shard_map/all_to_all | solution.py:382
  84.4 0.0 copy-done
  84.4 0.0 copy-done.1
  84.4 1.8 %far_field.1 = bf16[64,2048]{1,0:T(8,128)(2,1)} custom-call(bf16[16,16,640]{2,1,0:T(8,128)(2,1)S(1)} %all_to_all.10.msg, bf16[2048,128]{1,0:T(8,128)(2,1)S(1)} %copy-done.1, bf16[30,128,128]{2,1,0:T(8,128)(2,1)S(1)} %bitcast.5), custom_call_target="tpu_custom_call" | custom-call | tf_op jit(solution)/shard_map/far_field/pallas_call | solution.py:383
  (1 shorter events, 0.0 us)
Async XLA Ops:
  3.3 27.3 %all-to-all-start = ((bf16[16,16,1024]{2,1,0:T(8,128)(2,1)}), bf16[16,16,1024]{2,1,0:T(8,128)(2,1)S(1)}, u32[]{:S(2)}, u32[]{:S(2)}) async-start(bf16[16,16,1024]{2,1,0:T(8,128)(2,1)} %leaf_panels.1), calls=%async_computation | async-start | bytes 1048576 | tf_op jit(solution)/shard_map/all_to_all | solution.py:326
  13.2 13.6 %collective-permute-start.3 = (bf16[16,128,128]{2,1,0:T(8,128)(2,1)}, bf16[16,128,128]{2,1,0:T(8,128)(2,1)S(1)}, u32[]{:S(2)}, u32[]{:S(2)}) collective-permute-start(bf16[16,128,128]{2,1,0:T(8,128)(2,1)} %t0.1), channel_id=1, source_target_pairs={{0,1},{1,0},{2,3},{3,2},{4,5},{5,4},{6,7},{7,6},{8,9},{9,8},{10,11... | collective-permute-start | bytes 1572872 | tf_op jit(solution)/shard_map/ppermute | solution.py:315
  14.5 34.1 %collective-permute-start.5 = (bf16[16,128,128]{2,1,0:T(8,128)(2,1)}, bf16[16,128,128]{2,1,0:T(8,128)(2,1)S(1)}, u32[]{:S(2)}, u32[]{:S(2)}) collective-permute-start(bf16[16,128,128]{2,1,0:T(8,128)(2,1)} %t0.1), channel_id=1, source_target_pairs={{0,3},{1,2},{2,1},{3,0},{4,7},{5,6},{6,5},{7,4},{8,11},{9,10},{10,... | collective-permute-start | bytes 1572872 | tf_op jit(solution)/shard_map/ppermute | solution.py:316
  26.8 21.9 %collective-permute-start.4 = (bf16[16,128,128]{2,1,0:T(8,128)(2,1)S(1)}, bf16[16,128,128]{2,1,0:T(8,128)(2,1)S(1)}, u32[]{:S(2)}, u32[]{:S(2)}) collective-permute-start(bf16[16,128,128]{2,1,0:T(8,128)(2,1)S(1)} %collective-permute-done.3.t1), channel_id=1, source_target_pairs={{0,3},{1,2},{2,1},{3,0},{4,7},{5,6},{6,5},{7,4},{8,11},{9,10},{10,... | collective-permute-start | bytes 1572872 | tf_op jit(solution)/shard_map/ppermute | solution.py:353
  30.6 18.1 %copy-start.2 = (bf16[120,128,128]{2,1,0:T(8,128)(2,1)S(1)}, bf16[120,128,128]{2,1,0:T(8,128)(2,1)}, u32[]{:S(2)}) copy-start(bf16[120,128,128]{2,1,0:T(8,128)(2,1)} %tt.1) | copy-start | bytes 11796484
  30.6 18.1 %copy-start.3 = (bf16[16,128,128]{2,1,0:T(8,128)(2,1)S(1)}, bf16[16,128,128]{2,1,0:T(8,128)(2,1)}, u32[]{:S(2)}) copy-start(bf16[16,128,128]{2,1,0:T(8,128)(2,1)} %t0.1) | copy-start | bytes 1572868
  30.6 18.1 %copy-start.4 = (bf16[4,1024,256]{2,1,0:T(8,128)(2,1)S(1)}, bf16[4,1024,256]{2,1,0:T(8,128)(2,1)}, u32[]{:S(2)}) copy-start(bf16[4,1024,256]{2,1,0:T(8,128)(2,1)} %get-tuple-element.9.sel) | copy-start | bytes 6291460
  30.6 18.1 %copy-start.5 = (bf16[3072,128]{1,0:T(8,128)(2,1)S(1)}, bf16[3072,128]{1,0:T(8,128)(2,1)}, u32[]{:S(2)}) copy-start(bf16[3072,128]{1,0:T(8,128)(2,1)} %get-tuple-element.11.top_counts) | copy-start | bytes 2359300
  30.7 18.0 %collective-permute-start = (bf16[272,512]{1,0:T(8,128)(2,1)S(1)}, bf16[272,512]{1,0:T(8,128)(2,1)S(1)}, u32[]{:S(2)}, u32[]{:S(2)}) collective-permute-start(bf16[272,512]{1,0:T(8,128)(2,1)S(1)} %pack.1.a0), channel_id=1, source_target_pairs={{0,8},{8,16},{16,24},{24,0},{1,9},{9,17},{17,25},{25,1},{2,10},{10... | collective-permute-start | bytes 835592 | tf_op jit(solution)/shard_map/ppermute | solution.py:337
  31.9 16.7 %collective-permute-start.1 = (bf16[272,512]{1,0:T(8,128)(2,1)S(1)}, bf16[272,512]{1,0:T(8,128)(2,1)S(1)}, u32[]{:S(2)}, u32[]{:S(2)}) collective-permute-start(bf16[272,512]{1,0:T(8,128)(2,1)S(1)} %pack.1.a0), channel_id=1, source_target_pairs={{0,16},{8,24},{16,0},{24,8},{1,17},{9,25},{17,1},{25,9},{2,18},{10... | collective-permute-start | bytes 835592 | tf_op jit(solution)/shard_map/ppermute | solution.py:337
  34.4 14.3 %collective-permute-start.2 = (bf16[272,512]{1,0:T(8,128)(2,1)S(1)}, bf16[272,512]{1,0:T(8,128)(2,1)S(1)}, u32[]{:S(2)}, u32[]{:S(2)}) collective-permute-start(bf16[272,512]{1,0:T(8,128)(2,1)S(1)} %pack.1.a0), channel_id=1, source_target_pairs={{0,24},{8,0},{16,8},{24,16},{1,25},{9,1},{17,9},{25,17},{2,26},{10... | collective-permute-start | bytes 835592 | tf_op jit(solution)/shard_map/ppermute | solution.py:337
  48.7 35.7 %copy-start = (bf16[1,30,128,128]{3,2,1,0:T(8,128)(2,1)S(1)}, bf16[1,30,128,128]{3,2,1,0:T(8,128)(2,1)}, u32[]{:S(2)}) copy-start(bf16[1,30,128,128]{3,2,1,0:T(8,128)(2,1)} %param.10) | copy-start | bytes 2949124
  48.8 35.7 %copy-start.1 = (bf16[2048,128]{1,0:T(8,128)(2,1)S(1)}, bf16[2048,128]{1,0:T(8,128)(2,1)}, u32[]{:S(2)}) copy-start(bf16[2048,128]{1,0:T(8,128)(2,1)} %basis.3) | copy-start | bytes 1572868

commit v5 on v4

--- a/solution.py
+++ b/solution.py
@@ -192,7 +192,7 @@
             zs[m * CHUNK : (m + 1) * CHUNK, d] = z.reshape(CHUNK, 16, LANES)
         return carry
 
-    lax.fori_loop(0, GROUP, device, 0, unroll=2)
+    lax.fori_loop(0, GROUP, device, 0, unroll=4)
     for s in range(4):
         for r in range(ROWS):
             root[0:GROUP, :] = held[s][256:272, r * RANK : (r + 1) * RANK].astype(F32)

time: 86.4 us -> 85.8 us (level)
  no operation moved by 1% of the time
where the time goes in v5:
time: 85.8 us; the launch traced here: 85.5 us
  Pallas kernels  35.7 us (42%)
  starting transfers between devices  20.8 us (24%)
  blocking collectives  20.8 us (24%)
  waiting for transfers between devices  8.01 us (9%)
    all_to_all x1, blocking collectives, shards(): back = lax.all_to_all(back, ('z', 'core'), 0, 0, tiled=True)  20.8 us
    pallas_call x1, Pallas kernels, shards(): pl.pallas_call(couple_kernel, out_shape=jax.ShapeDtypeStruct((GROUP, LD,...  14.2 us
    pallas_call x1, Pallas kernels, shards(): pl.pallas_call(tally_kernel, out_shape=jax.ShapeDtypeStruct((GROUP, 1024,...  13.1 us
    all_to_all x1, starting transfers between devices, shards(): msg = lax.all_to_all(msg, ('z', 'core'), 0, 0, tiled=True)  9.98 us
    ppermute x1, waiting for transfers between devices, shards(): near = lax.ppermute(coupling_tiles, 'rhs', [(i, i ^ 1) for i in range(4)])  6.97 us
    ppermute x3, starting transfers between devices, shards(): lax.ppermute(mine, 'x', [(i, (i + s) % 4) for i in range(4)])  4.9 us
    pallas_call x1, Pallas kernels, shards(): pl.pallas_call(choice_kernel, out_shape=(jax.ShapeDtypeStruct((4, 1024, 2...  3.38 us
    pallas_call x1, Pallas kernels, shards(): pl.pallas_call(gather_kernel, out_shape=jax.ShapeDtypeStruct((GROUP, LD,...  3.26 us
  transfers between devices with their start and end apart: 7, of which 2 were waited for; matrix products, arithmetic and copies ran while one was open for 0% of the time, Pallas kernels for 19%

profile of v5, /device:TPU:1, one launch (start us, length us, event | category | flops | bytes accessed | tf_op | source)
XLA Modules:
  0.0 85.5 jit_solution(3393967410204264068)
XLA Ops:
  0.0 3.3 %leaf_panels.1 = bf16[16,16,1024]{2,1,0:T(8,128)(2,1)} custom-call(s32[1]{0:T(128)} %bitcast.xme, bf16[64,2048]{1,0:T(8,128)(2,1)} %rhs.1, bf16[2048,128]{1,0:T(8,128)(2,1)} %basis.3, bf16[30,128,128]{2,1,0:T(8,128)(2,1)} %bitcast.4, s32[2,16,192]{2,1,0:T(8,128)} %lists.1), custom_call_target="tpu_custom_call" | custom-call | tf_op jit(solution)/shard_map/leaf_panels/pallas_call | solution.py:317
  3.3 10.0 %all-to-all-start = ((bf16[16,16,1024]{2,1,0:T(8,128)(2,1)}), bf16[16,16,1024]{2,1,0:T(8,128)(2,1)S(1)}, u32[]{:S(2)}, u32[]{:S(2)}) async-start(bf16[16,16,1024]{2,1,0:T(8,128)(2,1)} %leaf_panels.1), calls=%async_computation | async-start | bytes 1048576 | tf_op jit(solution)/shard_map/all_to_all | solution.py:326
  13.2 1.3 %collective-permute-start.3 = (bf16[16,128,128]{2,1,0:T(8,128)(2,1)}, bf16[16,128,128]{2,1,0:T(8,128)(2,1)S(1)}, u32[]{:S(2)}, u32[]{:S(2)}) collective-permute-start(bf16[16,128,128]{2,1,0:T(8,128)(2,1)} %t0.1), channel_id=1, source_target_pairs={{0,1},{1,0},{2,3},{3,2},{4,5},{5,4},{6,7},{7,6},{8,9},{9,8},{10,11... | collective-permute-start | bytes 1572872 | tf_op jit(solution)/shard_map/ppermute | solution.py:315
  14.5 1.9 %collective-permute-start.5 = (bf16[16,128,128]{2,1,0:T(8,128)(2,1)}, bf16[16,128,128]{2,1,0:T(8,128)(2,1)S(1)}, u32[]{:S(2)}, u32[]{:S(2)}) collective-permute-start(bf16[16,128,128]{2,1,0:T(8,128)(2,1)} %t0.1), channel_id=1, source_target_pairs={{0,3},{1,2},{2,1},{3,0},{4,7},{5,6},{6,5},{7,4},{8,11},{9,10},{10,... | collective-permute-start | bytes 1572872 | tf_op jit(solution)/shard_map/ppermute | solution.py:316
  16.4 3.4 %choices.1 = (bf16[4,1024,256]{2,1,0:T(8,128)(2,1)}, bf16[3072,128]{1,0:T(8,128)(2,1)}) custom-call(s32[1]{0:T(128)} %bitcast.xme, s32[64,4,64]{2,1,0:T(4,128)} %bitcast.6, s32[3,512]{1,0:T(4,128)} %top.1), custom_call_target="tpu_custom_call" | custom-call | flops 400000000 | bytes 3000000 | tf_op jit(solution)/shard_map/choices/pallas_call | solution.py:339
  19.8 7.0 %collective-permute-done.3.t1 = bf16[16,128,128]{2,1,0:T(8,128)(2,1)S(1)} collective-permute-done((bf16[16,128,128]{2,1,0:T(8,128)(2,1)}, bf16[16,128,128]{2,1,0:T(8,128)(2,1)S(1)}, u32[]{:S(2)}, u32[]{:S(2)}) %collective-permute-start.3) | collective-permute-done | bytes 524320 | tf_op jit(solution)/shard_map/ppermute | solution.py:315
  26.8 2.7 %collective-permute-start.4 = (bf16[16,128,128]{2,1,0:T(8,128)(2,1)S(1)}, bf16[16,128,128]{2,1,0:T(8,128)(2,1)S(1)}, u32[]{:S(2)}, u32[]{:S(2)}) collective-permute-start(bf16[16,128,128]{2,1,0:T(8,128)(2,1)S(1)} %collective-permute-done.3.t1), channel_id=1, source_target_pairs={{0,3},{1,2},{2,1},{3,0},{4,7},{5,6},{6,5},{7,4},{8,11},{9,10},{10,... | collective-permute-start | bytes 1572872 | tf_op jit(solution)/shard_map/ppermute | solution.py:353
  29.5 1.0 %all-to-all-done.msg.lists = bf16[16,16,1024]{2,1,0:T(8,128)(2,1)S(1)} async-done(((bf16[16,16,1024]{2,1,0:T(8,128)(2,1)}), bf16[16,16,1024]{2,1,0:T(8,128)(2,1)S(1)}, u32[]{:S(2)}, u32[]{:S(2)}) %all-to-all-start) | async-done | bytes 524320 | tf_op jit(solution)/shard_map/all_to_all | solution.py:326
  30.6 0.0 copy-start.2
  30.6 0.0 copy-start.3
  30.6 0.0 copy-start.4
  30.6 0.0 copy-start.5
  30.7 1.3 %collective-permute-start = (bf16[272,512]{1,0:T(8,128)(2,1)S(1)}, bf16[272,512]{1,0:T(8,128)(2,1)S(1)}, u32[]{:S(2)}, u32[]{:S(2)}) collective-permute-start(bf16[272,512]{1,0:T(8,128)(2,1)S(1)} %pack.1.a0), channel_id=1, source_target_pairs={{0,8},{8,16},{16,24},{24,0},{1,9},{9,17},{17,25},{25,1},{2,10},{10... | collective-permute-start | bytes 835592 | tf_op jit(solution)/shard_map/ppermute | solution.py:337
  31.9 2.5 %collective-permute-start.1 = (bf16[272,512]{1,0:T(8,128)(2,1)S(1)}, bf16[272,512]{1,0:T(8,128)(2,1)S(1)}, u32[]{:S(2)}, u32[]{:S(2)}) collective-permute-start(bf16[272,512]{1,0:T(8,128)(2,1)S(1)} %pack.1.a0), channel_id=1, source_target_pairs={{0,16},{8,24},{16,0},{24,8},{1,17},{9,25},{17,1},{25,9},{2,18},{10... | collective-permute-start | bytes 835592 | tf_op jit(solution)/shard_map/ppermute | solution.py:337
  34.4 1.2 %collective-permute-start.2 = (bf16[272,512]{1,0:T(8,128)(2,1)S(1)}, bf16[272,512]{1,0:T(8,128)(2,1)S(1)}, u32[]{:S(2)}, u32[]{:S(2)}) collective-permute-start(bf16[272,512]{1,0:T(8,128)(2,1)S(1)} %pack.1.a0), channel_id=1, source_target_pairs={{0,24},{8,0},{16,8},{24,16},{1,25},{9,1},{17,9},{25,17},{2,26},{10... | collective-permute-start | bytes 835592 | tf_op jit(solution)/shard_map/ppermute | solution.py:337
  35.5 13.1 %tallies.1.counts = bf16[16,1024,256]{2,1,0:T(8,128)(2,1)S(1)} custom-call(bf16[16,16,1024]{2,1,0:T(8,128)(2,1)S(1)} %all-to-all-done.msg.lists), custom_call_target="tpu_custom_call" | custom-call | flops 4000000000 | bytes 12000000 | tf_op jit(solution)/shard_map/tallies/pallas_call | solution.py:355
  48.6 0.0 collective-permute-done.5.t3
  48.7 0.0 collective-permute-done.4.t2
  48.7 0.0 collective-permute-done.a1
  48.7 0.0 collective-permute-done.1.a2
  48.7 0.0 collective-permute-done.2.a3
  48.7 0.0 copy-done.2
  48.7 0.0 copy-done.3
  48.7 0.0 copy-done.4
  48.7 0.0 copy-done.5
  48.7 0.0 copy-start
  48.8 0.0 copy-start.1
  48.8 14.2 %interactions.1 = bf16[16,16,640]{2,1,0:T(8,128)(2,1)S(1)} custom-call(s32[1]{0:T(128)} %bitcast.xme, s32[1]{0:T(128)} %bitcast.1.yme, bf16[272,512]{1,0:T(8,128)(2,1)S(1)} %pack.1.a0, bf16[272,512]{1,0:T(8,128)(2,1)S(1)} %collective-permute-done.a1, bf16[272,512]{1,0:T(8,128)(2,1)S(1)} %collective-permute-done.1.a2, ...), custom_call_target="tpu_custom_call" | custom-call | flops 8000000000 | bytes 20000000 | tf_op jit(solution)/shard_map/interactions/pallas_call | solution.py:366
  62.9 20.8 %all_to_all.10.msg = bf16[16,16,640]{2,1,0:T(8,128)(2,1)S(1)} all-to-all(bf16[16,16,640]{2,1,0:T(8,128)(2,1)S(1)} %interactions.1), channel_id=1, replica_groups=mesh['z'=8,'x'=4,'core'=2,'rhs'=4] {'z','core'}, dimensions={0} | all-to-all | bytes 655360 | tf_op jit(solution)/shard_map/all_to_all | solution.py:382
  83.7 0.0 copy-done
  83.7 0.0 copy-done.1
  83.7 1.8 %far_field.1 = bf16[64,2048]{1,0:T(8,128)(2,1)} custom-call(bf16[16,16,640]{2,1,0:T(8,128)(2,1)S(1)} %all_to_all.10.msg, bf16[2048,128]{1,0:T(8,128)(2,1)S(1)} %copy-done.1, bf16[30,128,128]{2,1,0:T(8,128)(2,1)S(1)} %bitcast.5), custom_call_target="tpu_custom_call" | custom-call | tf_op jit(solution)/shard_map/far_field/pallas_call | solution.py:383
  (1 shorter events, 0.0 us)
Async XLA Ops:
  3.3 27.3 %all-to-all-start = ((bf16[16,16,1024]{2,1,0:T(8,128)(2,1)}), bf16[16,16,1024]{2,1,0:T(8,128)(2,1)S(1)}, u32[]{:S(2)}, u32[]{:S(2)}) async-start(bf16[16,16,1024]{2,1,0:T(8,128)(2,1)} %leaf_panels.1), calls=%async_computation | async-start | bytes 1048576 | tf_op jit(solution)/shard_map/all_to_all | solution.py:326
  13.2 13.6 %collective-permute-start.3 = (bf16[16,128,128]{2,1,0:T(8,128)(2,1)}, bf16[16,128,128]{2,1,0:T(8,128)(2,1)S(1)}, u32[]{:S(2)}, u32[]{:S(2)}) collective-permute-start(bf16[16,128,128]{2,1,0:T(8,128)(2,1)} %t0.1), channel_id=1, source_target_pairs={{0,1},{1,0},{2,3},{3,2},{4,5},{5,4},{6,7},{7,6},{8,9},{9,8},{10,11... | collective-permute-start | bytes 1572872 | tf_op jit(solution)/shard_map/ppermute | solution.py:315
  14.5 34.1 %collective-permute-start.5 = (bf16[16,128,128]{2,1,0:T(8,128)(2,1)}, bf16[16,128,128]{2,1,0:T(8,128)(2,1)S(1)}, u32[]{:S(2)}, u32[]{:S(2)}) collective-permute-start(bf16[16,128,128]{2,1,0:T(8,128)(2,1)} %t0.1), channel_id=1, source_target_pairs={{0,3},{1,2},{2,1},{3,0},{4,7},{5,6},{6,5},{7,4},{8,11},{9,10},{10,... | collective-permute-start | bytes 1572872 | tf_op jit(solution)/shard_map/ppermute | solution.py:316
  26.8 21.9 %collective-permute-start.4 = (bf16[16,128,128]{2,1,0:T(8,128)(2,1)S(1)}, bf16[16,128,128]{2,1,0:T(8,128)(2,1)S(1)}, u32[]{:S(2)}, u32[]{:S(2)}) collective-permute-start(bf16[16,128,128]{2,1,0:T(8,128)(2,1)S(1)} %collective-permute-done.3.t1), channel_id=1, source_target_pairs={{0,3},{1,2},{2,1},{3,0},{4,7},{5,6},{6,5},{7,4},{8,11},{9,10},{10,... | collective-permute-start | bytes 1572872 | tf_op jit(solution)/shard_map/ppermute | solution.py:353
  30.6 18.1 %copy-start.2 = (bf16[120,128,128]{2,1,0:T(8,128)(2,1)S(1)}, bf16[120,128,128]{2,1,0:T(8,128)(2,1)}, u32[]{:S(2)}) copy-start(bf16[120,128,128]{2,1,0:T(8,128)(2,1)} %tt.1) | copy-start | bytes 11796484
  30.6 18.1 %copy-start.3 = (bf16[16,128,128]{2,1,0:T(8,128)(2,1)S(1)}, bf16[16,128,128]{2,1,0:T(8,128)(2,1)}, u32[]{:S(2)}) copy-start(bf16[16,128,128]{2,1,0:T(8,128)(2,1)} %t0.1) | copy-start | bytes 1572868
  30.6 18.1 %copy-start.4 = (bf16[4,1024,256]{2,1,0:T(8,128)(2,1)S(1)}, bf16[4,1024,256]{2,1,0:T(8,128)(2,1)}, u32[]{:S(2)}) copy-start(bf16[4,1024,256]{2,1,0:T(8,128)(2,1)} %get-tuple-element.9.sel) | copy-start | bytes 6291460
  30.6 18.1 %copy-start.5 = (bf16[3072,128]{1,0:T(8,128)(2,1)S(1)}, bf16[3072,128]{1,0:T(8,128)(2,1)}, u32[]{:S(2)}) copy-start(bf16[3072,128]{1,0:T(8,128)(2,1)} %get-tuple-element.11.top_counts) | copy-start | bytes 2359300
  30.7 18.0 %collective-permute-start = (bf16[272,512]{1,0:T(8,128)(2,1)S(1)}, bf16[272,512]{1,0:T(8,128)(2,1)S(1)}, u32[]{:S(2)}, u32[]{:S(2)}) collective-permute-start(bf16[272,512]{1,0:T(8,128)(2,1)S(1)} %pack.1.a0), channel_id=1, source_target_pairs={{0,8},{8,16},{16,24},{24,0},{1,9},{9,17},{17,25},{25,1},{2,10},{10... | collective-permute-start | bytes 835592 | tf_op jit(solution)/shard_map/ppermute | solution.py:337
  31.9 16.7 %collective-permute-start.1 = (bf16[272,512]{1,0:T(8,128)(2,1)S(1)}, bf16[272,512]{1,0:T(8,128)(2,1)S(1)}, u32[]{:S(2)}, u32[]{:S(2)}) collective-permute-start(bf16[272,512]{1,0:T(8,128)(2,1)S(1)} %pack.1.a0), channel_id=1, source_target_pairs={{0,16},{8,24},{16,0},{24,8},{1,17},{9,25},{17,1},{25,9},{2,18},{10... | collective-permute-start | bytes 835592 | tf_op jit(solution)/shard_map/ppermute | solution.py:337
  34.4 14.3 %collective-permute-start.2 = (bf16[272,512]{1,0:T(8,128)(2,1)S(1)}, bf16[272,512]{1,0:T(8,128)(2,1)S(1)}, u32[]{:S(2)}, u32[]{:S(2)}) collective-permute-start(bf16[272,512]{1,0:T(8,128)(2,1)S(1)} %pack.1.a0), channel_id=1, source_target_pairs={{0,24},{8,0},{16,8},{24,16},{1,25},{9,1},{17,9},{25,17},{2,26},{10... | collective-permute-start | bytes 835592 | tf_op jit(solution)/shard_map/ppermute | solution.py:337
  48.7 35.0 %copy-start = (bf16[1,30,128,128]{3,2,1,0:T(8,128)(2,1)S(1)}, bf16[1,30,128,128]{3,2,1,0:T(8,128)(2,1)}, u32[]{:S(2)}) copy-start(bf16[1,30,128,128]{3,2,1,0:T(8,128)(2,1)} %param.10) | copy-start | bytes 2949124
  48.8 35.0 %copy-start.1 = (bf16[2048,128]{1,0:T(8,128)(2,1)S(1)}, bf16[2048,128]{1,0:T(8,128)(2,1)}, u32[]{:S(2)}) copy-start(bf16[2048,128]{1,0:T(8,128)(2,1)} %basis.3) | copy-start | bytes 1572868

commit v6 on v5

--- a/solution.py
+++ b/solution.py
@@ -148,7 +148,7 @@
         device(2 * i + 1, low1, high1, low0, high0)
         return carry
 
-    lax.fori_loop(0, GROUP // 2, two, 0)
+    lax.fori_loop(0, GROUP // 2, two, 0, unroll=2)
     for g in range(LD):
         settle(low1, high1, GROUP - 1, g)
 

time: 85.8 us -> 86.8 us (1.012)
  Pallas kernels: 35.7 us -> 36.7 us
    pallas_call x1, Pallas kernels: 13.1 us -> 14.2 us  [shards(): pl.pallas_call(tally_kernel, out_shape=jax.ShapeDtypeStruct((GROUP, 1024,...]
  transfers between devices with their start and end apart: 7 -> 7, of which waited for: 2 -> 2; matrix products, arithmetic and copies ran while one was open for 0% -> 0% of each run, Pallas kernels for 19% -> 20%
where the time goes in v6:
time: 86.8 us; the launch traced here: 86.6 us
  Pallas kernels  36.7 us (42%)
  starting transfers between devices  20.8 us (24%)
  blocking collectives  20.8 us (24%)
  waiting for transfers between devices  8.01 us (9%)
    all_to_all x1, blocking collectives, shards(): back = lax.all_to_all(back, ('z', 'core'), 0, 0, tiled=True)  20.8 us
    pallas_call x1, Pallas kernels, shards(): pl.pallas_call(tally_kernel, out_shape=jax.ShapeDtypeStruct((GROUP, 1024,...  14.2 us
    pallas_call x1, Pallas kernels, shards(): pl.pallas_call(couple_kernel, out_shape=jax.ShapeDtypeStruct((GROUP, LD,...  14.2 us
    all_to_all x1, starting transfers between devices, shards(): msg = lax.all_to_all(msg, ('z', 'core'), 0, 0, tiled=True)  9.98 us
    ppermute x1, waiting for transfers between devices, shards(): near = lax.ppermute(coupling_tiles, 'rhs', [(i, i ^ 1) for i in range(4)])  6.97 us
    ppermute x3, starting transfers between devices, shards(): lax.ppermute(mine, 'x', [(i, (i + s) % 4) for i in range(4)])  4.9 us
    pallas_call x1, Pallas kernels, shards(): pl.pallas_call(choice_kernel, out_shape=(jax.ShapeDtypeStruct((4, 1024, 2...  3.38 us
    pallas_call x1, Pallas kernels, shards(): pl.pallas_call(gather_kernel, out_shape=jax.ShapeDtypeStruct((GROUP, LD,...  3.26 us
  transfers between devices with their start and end apart: 7, of which 2 were waited for; matrix products, arithmetic and copies ran while one was open for 0% of the time, Pallas kernels for 20%

profile of v6, /device:TPU:1, one launch (start us, length us, event | category | flops | bytes accessed | tf_op | source)
XLA Modules:
  0.0 86.6 jit_solution(17461655954358239447)
XLA Ops:
  0.0 3.3 %leaf_panels.1 = bf16[16,16,1024]{2,1,0:T(8,128)(2,1)} custom-call(s32[1]{0:T(128)} %bitcast.xme, bf16[64,2048]{1,0:T(8,128)(2,1)} %rhs.1, bf16[2048,128]{1,0:T(8,128)(2,1)} %basis.3, bf16[30,128,128]{2,1,0:T(8,128)(2,1)} %bitcast.4, s32[2,16,192]{2,1,0:T(8,128)} %lists.1), custom_call_target="tpu_custom_call" | custom-call | tf_op jit(solution)/shard_map/leaf_panels/pallas_call | solution.py:317
  3.3 10.0 %all-to-all-start = ((bf16[16,16,1024]{2,1,0:T(8,128)(2,1)}), bf16[16,16,1024]{2,1,0:T(8,128)(2,1)S(1)}, u32[]{:S(2)}, u32[]{:S(2)}) async-start(bf16[16,16,1024]{2,1,0:T(8,128)(2,1)} %leaf_panels.1), calls=%async_computation | async-start | bytes 1048576 | tf_op jit(solution)/shard_map/all_to_all | solution.py:326
  13.2 1.3 %collective-permute-start.3 = (bf16[16,128,128]{2,1,0:T(8,128)(2,1)}, bf16[16,128,128]{2,1,0:T(8,128)(2,1)S(1)}, u32[]{:S(2)}, u32[]{:S(2)}) collective-permute-start(bf16[16,128,128]{2,1,0:T(8,128)(2,1)} %t0.1), channel_id=1, source_target_pairs={{0,1},{1,0},{2,3},{3,2},{4,5},{5,4},{6,7},{7,6},{8,9},{9,8},{10,11... | collective-permute-start | bytes 1572872 | tf_op jit(solution)/shard_map/ppermute | solution.py:315
  14.5 1.9 %collective-permute-start.5 = (bf16[16,128,128]{2,1,0:T(8,128)(2,1)}, bf16[16,128,128]{2,1,0:T(8,128)(2,1)S(1)}, u32[]{:S(2)}, u32[]{:S(2)}) collective-permute-start(bf16[16,128,128]{2,1,0:T(8,128)(2,1)} %t0.1), channel_id=1, source_target_pairs={{0,3},{1,2},{2,1},{3,0},{4,7},{5,6},{6,5},{7,4},{8,11},{9,10},{10,... | collective-permute-start | bytes 1572872 | tf_op jit(solution)/shard_map/ppermute | solution.py:316
  16.4 3.4 %choices.1 = (bf16[4,1024,256]{2,1,0:T(8,128)(2,1)}, bf16[3072,128]{1,0:T(8,128)(2,1)}) custom-call(s32[1]{0:T(128)} %bitcast.xme, s32[64,4,64]{2,1,0:T(4,128)} %bitcast.6, s32[3,512]{1,0:T(4,128)} %top.1), custom_call_target="tpu_custom_call" | custom-call | flops 400000000 | bytes 3000000 | tf_op jit(solution)/shard_map/choices/pallas_call | solution.py:339
  19.8 7.0 %collective-permute-done.3.t1 = bf16[16,128,128]{2,1,0:T(8,128)(2,1)S(1)} collective-permute-done((bf16[16,128,128]{2,1,0:T(8,128)(2,1)}, bf16[16,128,128]{2,1,0:T(8,128)(2,1)S(1)}, u32[]{:S(2)}, u32[]{:S(2)}) %collective-permute-start.3) | collective-permute-done | bytes 524320 | tf_op jit(solution)/shard_map/ppermute | solution.py:315
  26.8 2.7 %collective-permute-start.4 = (bf16[16,128,128]{2,1,0:T(8,128)(2,1)S(1)}, bf16[16,128,128]{2,1,0:T(8,128)(2,1)S(1)}, u32[]{:S(2)}, u32[]{:S(2)}) collective-permute-start(bf16[16,128,128]{2,1,0:T(8,128)(2,1)S(1)} %collective-permute-done.3.t1), channel_id=1, source_target_pairs={{0,3},{1,2},{2,1},{3,0},{4,7},{5,6},{6,5},{7,4},{8,11},{9,10},{10,... | collective-permute-start | bytes 1572872 | tf_op jit(solution)/shard_map/ppermute | solution.py:353
  29.5 1.0 %all-to-all-done.msg.lists = bf16[16,16,1024]{2,1,0:T(8,128)(2,1)S(1)} async-done(((bf16[16,16,1024]{2,1,0:T(8,128)(2,1)}), bf16[16,16,1024]{2,1,0:T(8,128)(2,1)S(1)}, u32[]{:S(2)}, u32[]{:S(2)}) %all-to-all-start) | async-done | bytes 524320 | tf_op jit(solution)/shard_map/all_to_all | solution.py:326
  30.6 0.0 copy-start.2
  30.6 0.0 copy-start.3
  30.6 0.0 copy-start.4
  30.6 0.0 copy-start.5
  30.7 1.3 %collective-permute-start = (bf16[272,512]{1,0:T(8,128)(2,1)S(1)}, bf16[272,512]{1,0:T(8,128)(2,1)S(1)}, u32[]{:S(2)}, u32[]{:S(2)}) collective-permute-start(bf16[272,512]{1,0:T(8,128)(2,1)S(1)} %pack.1.a0), channel_id=1, source_target_pairs={{0,8},{8,16},{16,24},{24,0},{1,9},{9,17},{17,25},{25,1},{2,10},{10... | collective-permute-start | bytes 835592 | tf_op jit(solution)/shard_map/ppermute | solution.py:337
  31.9 2.5 %collective-permute-start.1 = (bf16[272,512]{1,0:T(8,128)(2,1)S(1)}, bf16[272,512]{1,0:T(8,128)(2,1)S(1)}, u32[]{:S(2)}, u32[]{:S(2)}) collective-permute-start(bf16[272,512]{1,0:T(8,128)(2,1)S(1)} %pack.1.a0), channel_id=1, source_target_pairs={{0,16},{8,24},{16,0},{24,8},{1,17},{9,25},{17,1},{25,9},{2,18},{10... | collective-permute-start | bytes 835592 | tf_op jit(solution)/shard_map/ppermute | solution.py:337
  34.4 1.2 %collective-permute-start.2 = (bf16[272,512]{1,0:T(8,128)(2,1)S(1)}, bf16[272,512]{1,0:T(8,128)(2,1)S(1)}, u32[]{:S(2)}, u32[]{:S(2)}) collective-permute-start(bf16[272,512]{1,0:T(8,128)(2,1)S(1)} %pack.1.a0), channel_id=1, source_target_pairs={{0,24},{8,0},{16,8},{24,16},{1,25},{9,1},{17,9},{25,17},{2,26},{10... | collective-permute-start | bytes 835592 | tf_op jit(solution)/shard_map/ppermute | solution.py:337
  35.5 14.2 %tallies.1.counts = bf16[16,1024,256]{2,1,0:T(8,128)(2,1)S(1)} custom-call(bf16[16,16,1024]{2,1,0:T(8,128)(2,1)S(1)} %all-to-all-done.msg.lists), custom_call_target="tpu_custom_call" | custom-call | flops 4000000000 | bytes 12000000 | tf_op jit(solution)/shard_map/tallies/pallas_call | solution.py:355
  49.7 0.0 collective-permute-done.5.t3
  49.7 0.0 collective-permute-done.4.t2
  49.7 0.0 collective-permute-done.a1
  49.7 0.0 collective-permute-done.1.a2
  49.8 0.0 collective-permute-done.2.a3
  49.8 0.0 copy-done.2
  49.8 0.0 copy-done.3
  49.8 0.0 copy-done.4
  49.8 0.0 copy-done.5
  49.8 0.0 copy-start
  49.8 0.0 copy-start.1
  49.8 14.2 %interactions.1 = bf16[16,16,640]{2,1,0:T(8,128)(2,1)S(1)} custom-call(s32[1]{0:T(128)} %bitcast.xme, s32[1]{0:T(128)} %bitcast.1.yme, bf16[272,512]{1,0:T(8,128)(2,1)S(1)} %pack.1.a0, bf16[272,512]{1,0:T(8,128)(2,1)S(1)} %collective-permute-done.a1, bf16[272,512]{1,0:T(8,128)(2,1)S(1)} %collective-permute-done.1.a2, ...), custom_call_target="tpu_custom_call" | custom-call | flops 8000000000 | bytes 20000000 | tf_op jit(solution)/shard_map/interactions/pallas_call | solution.py:366
  64.0 20.8 %all_to_all.10.msg = bf16[16,16,640]{2,1,0:T(8,128)(2,1)S(1)} all-to-all(bf16[16,16,640]{2,1,0:T(8,128)(2,1)S(1)} %interactions.1), channel_id=1, replica_groups=mesh['z'=8,'x'=4,'core'=2,'rhs'=4] {'z','core'}, dimensions={0} | all-to-all | bytes 655360 | tf_op jit(solution)/shard_map/all_to_all | solution.py:382
  84.8 0.0 copy-done
  84.8 0.0 copy-done.1
  84.8 1.8 %far_field.1 = bf16[64,2048]{1,0:T(8,128)(2,1)} custom-call(bf16[16,16,640]{2,1,0:T(8,128)(2,1)S(1)} %all_to_all.10.msg, bf16[2048,128]{1,0:T(8,128)(2,1)S(1)} %copy-done.1, bf16[30,128,128]{2,1,0:T(8,128)(2,1)S(1)} %bitcast.5), custom_call_target="tpu_custom_call" | custom-call | tf_op jit(solution)/shard_map/far_field/pallas_call | solution.py:383
  (1 shorter events, 0.0 us)
Async XLA Ops:
  3.3 27.3 %all-to-all-start = ((bf16[16,16,1024]{2,1,0:T(8,128)(2,1)}), bf16[16,16,1024]{2,1,0:T(8,128)(2,1)S(1)}, u32[]{:S(2)}, u32[]{:S(2)}) async-start(bf16[16,16,1024]{2,1,0:T(8,128)(2,1)} %leaf_panels.1), calls=%async_computation | async-start | bytes 1048576 | tf_op jit(solution)/shard_map/all_to_all | solution.py:326
  13.2 13.6 %collective-permute-start.3 = (bf16[16,128,128]{2,1,0:T(8,128)(2,1)}, bf16[16,128,128]{2,1,0:T(8,128)(2,1)S(1)}, u32[]{:S(2)}, u32[]{:S(2)}) collective-permute-start(bf16[16,128,128]{2,1,0:T(8,128)(2,1)} %t0.1), channel_id=1, source_target_pairs={{0,1},{1,0},{2,3},{3,2},{4,5},{5,4},{6,7},{7,6},{8,9},{9,8},{10,11... | collective-permute-start | bytes 1572872 | tf_op jit(solution)/shard_map/ppermute | solution.py:315
  14.5 35.2 %collective-permute-start.5 = (bf16[16,128,128]{2,1,0:T(8,128)(2,1)}, bf16[16,128,128]{2,1,0:T(8,128)(2,1)S(1)}, u32[]{:S(2)}, u32[]{:S(2)}) collective-permute-start(bf16[16,128,128]{2,1,0:T(8,128)(2,1)} %t0.1), channel_id=1, source_target_pairs={{0,3},{1,2},{2,1},{3,0},{4,7},{5,6},{6,5},{7,4},{8,11},{9,10},{10,... | collective-permute-start | bytes 1572872 | tf_op jit(solution)/shard_map/ppermute | solution.py:316
  26.8 22.9 %collective-permute-start.4 = (bf16[16,128,128]{2,1,0:T(8,128)(2,1)S(1)}, bf16[16,128,128]{2,1,0:T(8,128)(2,1)S(1)}, u32[]{:S(2)}, u32[]{:S(2)}) collective-permute-start(bf16[16,128,128]{2,1,0:T(8,128)(2,1)S(1)} %collective-permute-done.3.t1), channel_id=1, source_target_pairs={{0,3},{1,2},{2,1},{3,0},{4,7},{5,6},{6,5},{7,4},{8,11},{9,10},{10,... | collective-permute-start | bytes 1572872 | tf_op jit(solution)/shard_map/ppermute | solution.py:353
  30.6 19.2 %copy-start.2 = (bf16[120,128,128]{2,1,0:T(8,128)(2,1)S(1)}, bf16[120,128,128]{2,1,0:T(8,128)(2,1)}, u32[]{:S(2)}) copy-start(bf16[120,128,128]{2,1,0:T(8,128)(2,1)} %tt.1) | copy-start | bytes 11796484
  30.6 19.2 %copy-start.3 = (bf16[16,128,128]{2,1,0:T(8,128)(2,1)S(1)}, bf16[16,128,128]{2,1,0:T(8,128)(2,1)}, u32[]{:S(2)}) copy-start(bf16[16,128,128]{2,1,0:T(8,128)(2,1)} %t0.1) | copy-start | bytes 1572868
  30.6 19.2 %copy-start.4 = (bf16[4,1024,256]{2,1,0:T(8,128)(2,1)S(1)}, bf16[4,1024,256]{2,1,0:T(8,128)(2,1)}, u32[]{:S(2)}) copy-start(bf16[4,1024,256]{2,1,0:T(8,128)(2,1)} %get-tuple-element.9.sel) | copy-start | bytes 6291460
  30.6 19.2 %copy-start.5 = (bf16[3072,128]{1,0:T(8,128)(2,1)S(1)}, bf16[3072,128]{1,0:T(8,128)(2,1)}, u32[]{:S(2)}) copy-start(bf16[3072,128]{1,0:T(8,128)(2,1)} %get-tuple-element.11.top_counts) | copy-start | bytes 2359300
  30.7 19.1 %collective-permute-start = (bf16[272,512]{1,0:T(8,128)(2,1)S(1)}, bf16[272,512]{1,0:T(8,128)(2,1)S(1)}, u32[]{:S(2)}, u32[]{:S(2)}) collective-permute-start(bf16[272,512]{1,0:T(8,128)(2,1)S(1)} %pack.1.a0), channel_id=1, source_target_pairs={{0,8},{8,16},{16,24},{24,0},{1,9},{9,17},{17,25},{25,1},{2,10},{10... | collective-permute-start | bytes 835592 | tf_op jit(solution)/shard_map/ppermute | solution.py:337
  31.9 17.8 %collective-permute-start.1 = (bf16[272,512]{1,0:T(8,128)(2,1)S(1)}, bf16[272,512]{1,0:T(8,128)(2,1)S(1)}, u32[]{:S(2)}, u32[]{:S(2)}) collective-permute-start(bf16[272,512]{1,0:T(8,128)(2,1)S(1)} %pack.1.a0), channel_id=1, source_target_pairs={{0,16},{8,24},{16,0},{24,8},{1,17},{9,25},{17,1},{25,9},{2,18},{10... | collective-permute-start | bytes 835592 | tf_op jit(solution)/shard_map/ppermute | solution.py:337
  34.4 15.4 %collective-permute-start.2 = (bf16[272,512]{1,0:T(8,128)(2,1)S(1)}, bf16[272,512]{1,0:T(8,128)(2,1)S(1)}, u32[]{:S(2)}, u32[]{:S(2)}) collective-permute-start(bf16[272,512]{1,0:T(8,128)(2,1)S(1)} %pack.1.a0), channel_id=1, source_target_pairs={{0,24},{8,0},{16,8},{24,16},{1,25},{9,1},{17,9},{25,17},{2,26},{10... | collective-permute-start | bytes 835592 | tf_op jit(solution)/shard_map/ppermute | solution.py:337
  49.8 35.0 %copy-start = (bf16[1,30,128,128]{3,2,1,0:T(8,128)(2,1)S(1)}, bf16[1,30,128,128]{3,2,1,0:T(8,128)(2,1)}, u32[]{:S(2)}) copy-start(bf16[1,30,128,128]{3,2,1,0:T(8,128)(2,1)} %param.10) | copy-start | bytes 2949124
  49.8 35.0 %copy-start.1 = (bf16[2048,128]{1,0:T(8,128)(2,1)S(1)}, bf16[2048,128]{1,0:T(8,128)(2,1)}, u32[]{:S(2)}) copy-start(bf16[2048,128]{1,0:T(8,128)(2,1)} %basis.3) | copy-start | bytes 1572868
